TPU v7x, 128 devices: a whole 4x4x4 slice. The times are simulated.
128 devices in a mesh: ga: 4 (over z), dev: 32 (over y, x, core).
Axes of the slice: x: 4, y: 4, z: 4, core: 2. Of those that a mesh axis runs over, the one named last changes fastest.
Arguments:
- density: float32 [4, 1024, 1024], P(None, 'dev', 'ga'), may hold values from 1 to 2
- velocity: float32 [3, 4, 1024, 1024], P(None, None, 'dev', 'ga'), may hold values from -2.5 to 2.5
- pressure: float32 [4, 1024, 1024], P(None, 'dev', 'ga'), may hold values from 2 to 4
- lift: bfloat16 [3, 32], replicated, may hold values from -32 to 32
- spectral: bfloat16 [64, 2, 32, 32, 128], P('dev'), may hold values from -6 to 6
- pointwise: bfloat16 [32, 32], replicated, may hold values from -1 to 1
- project: bfloat16 [32, 3], replicated, may hold values from -1 to 1
Outputs:
- new_state: float32 [5, 4, 1024, 1024], P(None, None, 'dev', 'ga')
- spectral_grad: float32 [64, 2, 32, 32, 128], P('dev')
All inputs are finite; a program needn't handle non-finite values.
Results may differ from a plain program's by a relative error of at most 0.0003.
Values sent between devices are 32-bit elements; how exact they have to be, the bound alone decides.
A program may use at most 128 MiB of HBM per device.

v0:
```python
import functools
import math

import jax
import jax.numpy as jnp
import numpy as np
from jax import lax
from jax.experimental import pallas as pl
from jax.experimental.pallas import tpu as pltpu
from jax.sharding import PartitionSpec as P

MESH = pl.DeviceIdType.MESH
F32 = jnp.float32
BF16 = jnp.bfloat16
WIDTH = 32
MODES = 64
XC = 512
YC = 512
GA = 4
DEV = 32
DT = 0.12


def tables():
    ky = np.arange(MODES)
    y = np.arange(YC)
    ang = 2 * np.pi * ((ky[:, None] * y[None, :]) % YC) / YC
    fwd = np.stack([np.cos(ang), -np.sin(ang)], axis=1)
    weight = np.where(ky == 0, 1.0, 2.0) / (XC * YC)
    inv = fwd * weight[:, None, None]
    fwd_dj = fwd.reshape(DEV, 4, YC)
    fwd_jd = fwd_dj.transpose(1, 0, 2).reshape(128, YC)
    inv_jd = inv.reshape(DEV, 4, YC).transpose(1, 0, 2).reshape(128, YC).T
    q = np.arange(2 * MODES)
    kx = np.where(q < MODES, q, XC - 2 * MODES + q)
    ax = 2 * np.pi * ((kx[:, None] * np.arange(XC)[None, :]) % XC) / XC
    cx = np.concatenate([np.cos(ax), np.sin(ax)], axis=0)

    def split(a):
        a = np.asarray(a, np.float32)
        hi = a.astype(jnp.bfloat16)
        lo = (a - hi.astype(np.float32)).astype(jnp.bfloat16)
        return np.ascontiguousarray(np.stack([hi, lo]))

    pool = np.zeros((256, 128), np.float32)
    pool[np.arange(256), np.arange(256) // 2] = 0.25
    return (
        split(fwd_dj.reshape(128, YC)),
        split(fwd_jd),
        split(inv_jd),
        split(cx),
        split(cx.T),
        pool.astype(jnp.bfloat16),
    )


def split2(a):
    hi = a.astype(BF16)
    return hi, (a - hi.astype(F32)).astype(BF16)


def nn(a, b):
    return lax.dot_general(a, b, (((1,), (0,)), ((), ())), preferred_element_type=F32)


def nt(a, b):
    return lax.dot_general(a, b, (((1,), (1,)), ((), ())), preferred_element_type=F32)


def tn(a, b):
    return lax.dot_general(a, b, (((0,), (0,)), ((), ())), preferred_element_type=F32)


def primitives(u):
    inv = 1.0 / u[0]
    v = [u[1] * inv, u[2] * inv, u[3] * inv]
    kinetic = u[1] * v[0] + u[2] * v[1] + u[3] * v[2]
    p = 0.4 * (u[4] - 0.5 * kinetic)
    sound = jnp.sqrt(1.4 * p * inv)
    return v, p, sound


def directional(u, v, p, sound, d):
    n = v[d]
    flux = [u[1 + d]]
    for i in range(3):
        f = u[1 + i] * n
        flux.append(f + p if i == d else f)
    flux.append((u[4] + p) * n)
    return flux, jnp.abs(n) + sound


def faces(ul, ur, fl, fr, sl, sr):
    top = jnp.maximum(sl, sr)
    return [(a + b) - top * (d - c) for a, b, c, d in zip(fl, fr, ul, ur)]


def rim_rates(u):
    v, p, sound = primitives(u)
    total, along_y = None, None
    for d, (axis, step, size) in enumerate(((0, 2, 8), (1, 8, 384), (1, 1, 384))):
        flux, speed = directional(u, v, p, sound, d)

        def up(a):
            return pltpu.roll(a, size - step, axis)

        g = faces(u, [up(a) for a in u], flux, [up(a) for a in flux], speed, up(speed))
        div = [a - pltpu.roll(a, step, axis) for a in g]
        total = div if total is None else [a + b for a, b in zip(total, div)]
        along_y = g
    return total, along_y


def block_rates(src, edge, r0):
    lane = lax.broadcasted_iota(jnp.int32, (4, 8, 128), 2)
    odd = lax.broadcasted_iota(jnp.int32, (4, 8, 128), 1) % 2 == 1
    last = lane == 127
    base = pl.multiple_of(8 * (r0 - 1), 8)
    wide = [src[f, pl.ds(base, 48), :].reshape(6, 8, 128) for f in range(5)]
    v, p, sound = primitives(wide)
    flux, speed = directional(wide, v, p, sound, 1)
    g = faces(
        [a[:5] for a in wide], [a[1:] for a in wide], [a[:5] for a in flux], [a[1:] for a in flux], speed[:5], speed[1:]
    )
    total = [a[1:] - a[:4] for a in g]
    u = [a[1:5] for a in wide]
    v = [a[1:5] for a in v]
    p, sound = p[1:5], sound[1:5]

    flux, speed = directional(u, v, p, sound, 0)

    def up_z(a):
        return pltpu.roll(a, 6, 1)

    g = faces(u, [up_z(a) for a in u], flux, [up_z(a) for a in flux], speed, up_z(speed))
    total = [t + (a - pltpu.roll(a, 2, 1)) for t, a in zip(total, g)]

    flux, speed = directional(u, v, p, sound, 2)

    def up_y(a):
        near = pltpu.roll(a, 127, 2)
        return jnp.where(last, pltpu.roll(near, 7, 1), near)

    g = faces(u, [up_y(a) for a in u], flux, [up_y(a) for a in flux], speed, up_y(speed))
    at = pl.multiple_of(8 * r0, 8)
    for f in range(5):
        outer = edge[f, pl.ds(at, 32), :].reshape(4, 8, 128)
        upper = jnp.where(last & odd, outer, g[f])
        wrapped = jnp.where(odd, pltpu.roll(g[f], 1, 1), outer)
        lower = pltpu.roll(jnp.where(last, wrapped, g[f]), 1, 2)
        total[f] = total[f] + (upper - lower)
    return total


def kernel(
    lift_s, density, velocity, pressure, lift, pointwise, project, spectral_h,
    fdj_h, fjd_h, inv_h, cx_h, cxt_h, pool_h,
    new_state, t_out,
    spectral, fdj, fjd, inv, cx, cxt, pool,
    u0, ua, ub, acc, edge, rim, own_edge, side_edge, row_edge, corner_edge,
    pooled, snd_in, rcv_in, snd_tg, rcv_tg, snd_x, rcv_x, snd_b, rcv_b, snd_g, rcv_g,
    contracted, modes, grads, rt_hi, rt_lo, slope, made, dp_hi, dp_lo, ft, lpx_ref, pxt_ref,
    load_sem, halo_send, halo_recv, in_send, in_recv, tg_send, tg_recv, x_send, x_recv, b_send, b_recv,
    g_send, g_recv, xm_send, xm_recv, gm_send, gm_recv,
):
    ga = lax.axis_index("ga")
    dev = lax.axis_index("dev")
    east, west = lax.rem(ga + 1, GA), lax.rem(ga + GA - 1, GA)
    south, north = lax.rem(dev + 1, DEV), lax.rem(dev + DEV - 1, DEV)

    loads = [
        pltpu.make_async_copy(a, b, load_sem.at[n])
        for n, (a, b) in enumerate(
            ((pool_h, pool), (spectral_h, spectral), (fdj_h, fdj), (cx_h, cx), (cxt_h, cxt), (inv_h, inv), (fjd_h, fjd))
        )
    ]
    for c in loads:
        c.start()

    barrier = pltpu.get_barrier_semaphore()

    def greet(s, carry):
        pl.semaphore_signal(barrier, inc=1, device_id=(ga, lax.rem(dev + s, DEV)), device_id_type=MESH)
        return carry

    lax.fori_loop(1, DEV, greet, 0)
    for s in range(1, GA):
        pl.semaphore_signal(barrier, inc=1, device_id=(lax.rem(ga + s, GA), dev), device_id_type=MESH)
    for a in (east, west):
        for b in (south, north):
            pl.semaphore_signal(barrier, inc=1, device_id=(a, b), device_id_type=MESH)

    def exchange_rows(snd, rcv, ssem, rsem):
        def go(s, carry):
            peer = lax.rem(dev + s, DEV)
            pltpu.make_async_remote_copy(
                src_ref=snd.at[pl.ds(pl.multiple_of(16 * peer, 16), 16)],
                dst_ref=rcv.at[pl.ds(pl.multiple_of(16 * dev, 16), 16)],
                send_sem=ssem.at[peer], recv_sem=rsem.at[dev],
                device_id=(ga, peer), device_id_type=MESH,
            ).start()
            return carry

        lax.fori_loop(1, DEV, go, 0)
        mine = pl.ds(pl.multiple_of(16 * dev, 16), 16)
        rcv[mine, :] = snd[mine, :]

    def wait_rows(snd, rcv, ssem, rsem):
        def go(s, carry):
            peer = lax.rem(dev + s, DEV)
            at = pl.ds(pl.multiple_of(16 * peer, 16), 16)
            pltpu.make_async_remote_copy(
                src_ref=snd.at[at], dst_ref=rcv.at[at], send_sem=ssem.at[peer], recv_sem=rsem.at[peer],
                device_id=(ga, peer), device_id_type=MESH,
            ).wait()
            return carry

        lax.fori_loop(1, DEV, go, 0)

    def across(s, src, dst, ssem, rsem, arriving):
        peer = lax.rem(ga + s, GA)
        return pltpu.make_async_remote_copy(
            src_ref=src(peer), dst_ref=dst(peer if arriving else ga), send_sem=ssem.at[peer],
            recv_sem=rsem.at[peer if arriving else ga], device_id=(peer, dev), device_id_type=MESH,
        )

    def start_across(src, dst, ssem, rsem):
        for s in (1, 3, 2):
            across(s, src, dst, ssem, rsem, False).start()

    def wait_across(src, dst, ssem, rsem):
        for s in (1, 3, 2):
            across(s, src, dst, ssem, rsem, True).wait()

    def coarsen(rows, snd):
        hi, lo = split2(rows)
        pooled[...] = nn(hi, pool[...]) + nn(lo, pool[...])
        both = pooled[pl.ds(0, 192, stride=2), :] + pooled[pl.ds(1, 192, stride=2), :]
        snd[...] = both.reshape(GA, 48, 128)

    for p in range(4):
        for h in range(2):
            cols = slice(128 * h, 128 * h + 128)
            rho = density[p, :, cols]
            v = [velocity[c, p, :, cols] for c in range(3)]
            where = pl.ds(32 + 2 * p + h, 32, stride=8)
            u0[0, where, :] = rho
            for c in range(3):
                u0[1 + c, where, :] = rho * v[c]
            u0[4, where, :] = pressure[p, :, cols] / 0.4 + 0.5 * rho * (v[0] * v[0] + v[1] * v[1] + v[2] * v[2])

    lane1 = lax.broadcasted_iota(jnp.int32, (8, 128), 1)
    for w in range(2):
        for f in range(5):
            packed = None
            for k in range(16):
                row = pltpu.roll(u0[f, pl.ds(8 * (16 * w + k + 4), 8), :], (4 + 8 * k) % 128, 1)
                packed = row if packed is None else jnp.where(lane1 >= 8 * k, row, packed)
            own_edge[w, f] = packed

    loads[0].wait()
    coarsen(jnp.concatenate([velocity[c, p] for p in range(4) for c in range(3)], axis=0), snd_in)

    pl.semaphore_wait(barrier, DEV - 1 + GA - 1 + 4)

    def halo(n, src, dst, target):
        return pltpu.make_async_remote_copy(
            src_ref=src, dst_ref=dst, send_sem=halo_send.at[n], recv_sem=halo_recv.at[n],
            device_id=target, device_id_type=MESH,
        )

    halos = [
        halo(0, u0.at[:, pl.ds(8 * 32, 32)], u0.at[:, pl.ds(0, 32)], (ga, south)),
        halo(1, u0.at[:, pl.ds(8 * 4, 32)], u0.at[:, pl.ds(8 * 36, 32)], (ga, north)),
        halo(2, own_edge.at[1], row_edge.at[0], (ga, south)),
        halo(3, own_edge.at[0], row_edge.at[1], (ga, north)),
        halo(4, own_edge, side_edge.at[0], (east, dev)),
        halo(5, own_edge, side_edge.at[1], (west, dev)),
        halo(6, own_edge.at[1], corner_edge.at[0], (east, south)),
        halo(7, own_edge.at[0], corner_edge.at[1], (east, north)),
        halo(8, own_edge.at[1], corner_edge.at[2], (west, south)),
        halo(9, own_edge.at[0], corner_edge.at[3], (west, north)),
    ]
    in_args = (lambda g: snd_in.at[g], lambda g: rcv_in.at[g], in_send, in_recv)
    start_across(*in_args)
    for c in halos:
        c.start()
    rcv_in[ga] = snd_in[ga]

    loads[1].wait()
    for ky in range(2):
        for part in range(2):

            def add(w8, total, ky=ky, part=part):
                total = list(total)
                for n in range(4):
                    w = 4 * w8 + n
                    s = spectral[ky, part, w].astype(F32)
                    for c in range(3):
                        total[c] = total[c] + lift_s[c, w] * s
                return tuple(total)

            zero = jnp.zeros((WIDTH, 128), F32)
            done = lax.fori_loop(0, WIDTH // 4, add, (zero, zero, zero))
            for c in range(3):
                contracted[ky, part, c] = done[c]

    tile_o = (
        lax.broadcasted_iota(jnp.int32, (WIDTH, 512), 1) % WIDTH == lax.broadcasted_iota(jnp.int32, (WIDTH, 512), 0)
    ).astype(F32).astype(BF16)
    same_row = (
        lax.broadcasted_iota(jnp.int32, (48, 512), 1) // WIDTH == lax.broadcasted_iota(jnp.int32, (48, 512), 0) % 16
    )

    def spread(a):
        return jnp.where(
            same_row, jnp.concatenate([jnp.broadcast_to(a[c : c + 1], (16, 512)) for c in range(3)], axis=0), 0.0
        )

    lp_hi, lp_lo = split2(nn(lift[...], pointwise[...]))
    lpx_ref[...] = spread(nn(lp_hi, tile_o) + nn(lp_lo, tile_o))
    pxt_ref[...] = spread(tn(project[...], tile_o)).astype(BF16)

    wait_across(*in_args)
    loads[2].wait()
    hi, lo = split2(jnp.concatenate([rcv_in[g] for g in range(GA)], axis=1))
    freq = nt(hi, fdj[0]) + nt(hi, fdj[1]) + nt(lo, fdj[0])
    lane2 = lax.broadcasted_iota(jnp.int32, (16, 128), 1)
    for d in range(DEV):
        a, b, c = (pltpu.roll(freq[16 * n : 16 * n + 16], (4 * n - 4 * d) % 128, 1) for n in range(3))
        snd_x[pl.ds(16 * d, 16), :] = jnp.where(lane2 < 4, a, jnp.where(lane2 < 8, b, c))
    x_args = (snd_x, rcv_x, x_send, x_recv)
    exchange_rows(*x_args)

    for c in halos:
        c.wait()
    sub1 = lax.broadcasted_iota(jnp.int32, (8, 128), 0)
    even, first = sub1 % 2 == 0, lane1 % 8 < 4
    low = lane1 < 64
    for f in range(5):
        own = [own_edge[0, f], own_edge[1, f], jnp.where(low, row_edge[1, f], row_edge[0, f])]
        left = [side_edge[0, 0, f], side_edge[0, 1, f], jnp.where(low, corner_edge[1, f], corner_edge[0, f])]
        right = [side_edge[1, 0, f], side_edge[1, 1, f], jnp.where(low, corner_edge[3, f], corner_edge[2, f])]
        for n in range(3):
            rim[0, f, :, 128 * n : 128 * n + 128] = jnp.where(
                even,
                jnp.where(first, pltpu.roll(left[n], 7, 0), own[n]),
                jnp.where(first, own[n], pltpu.roll(right[n], 1, 0)),
            )

    def stage(src, dst, ahead, gain, first_row, blocks, first_stage, rim_src, rim_dst):
        total, along_y = rim_rates([rim[rim_src, f] for f in range(5)])
        for f in range(5):
            if rim_dst is not None:
                rim[rim_dst, f] = rim[0, f] - (0.5 * ahead) * total[f]
            for n in range(3):
                for k in range(16):
                    edge[f, pl.ds(8 * ((16 * n + k + 4) % 48), 8), :] = pltpu.roll(
                        along_y[f][:, 128 * n : 128 * n + 128], 124 - 8 * k, 1
                    )

        def block(n, carry):
            r0 = first_row + 4 * n
            if first_stage:
                r0 = jnp.minimum(r0, 35)
            total = block_rates(src, edge, r0)
            at = pl.ds(pl.multiple_of(8 * r0, 8), 32)
            for f in range(5):
                t = total[f].reshape(32, 128)
                start = u0[f, at, :]
                if dst is not None:
                    dst[f, at, :] = start - (0.5 * ahead) * t
                old = start if first_stage else acc[f, at, :]
                acc[f, at, :] = old - (0.5 * gain) * t
            return carry

        lax.fori_loop(0, blocks, block, 0)

    stage(u0, ua, 0.5 * DT, DT / 6, 1, 10, True, 0, 1)

    wait_rows(*x_args)
    loads[3].wait()
    hi, lo = split2(rcv_x[...])
    turned = nn(cx[0], hi) + nn(cx[1], hi) + nn(cx[0], lo)
    cosine, sine = turned[:128].T, turned[128:].T
    for ky in range(2):
        for c in range(3):
            r = 4 * c + 2 * ky
            modes[ga, 8 * ky + 2 * c : 8 * ky + 2 * c + 1, :] = cosine[r : r + 1] + sine[r + 1 : r + 2]
            modes[ga, 8 * ky + 2 * c + 1 : 8 * ky + 2 * c + 2, :] = cosine[r + 1 : r + 2] - sine[r : r + 1]
        modes[ga, 8 * ky + 6 : 8 * ky + 8, :] = jnp.zeros((2, 128), F32)
    modes_args = (lambda g: modes.at[ga], lambda g: modes.at[g], xm_send, xm_recv)
    start_across(*modes_args)
    mine = modes[ga]
    rows = []
    for ky in range(2):
        out_re, out_im = 0.0, 0.0
        for c in range(3):
            a = mine[8 * ky + 2 * c : 8 * ky + 2 * c + 1]
            b = mine[8 * ky + 2 * c + 1 : 8 * ky + 2 * c + 2]
            re, im = contracted[ky, 0, c], contracted[ky, 1, c]
            out_re = out_re + (a * re - b * im)
            out_im = out_im + (a * im + b * re)
        rows.append(jnp.concatenate([out_re, -out_im], axis=1))
        rows.append(jnp.concatenate([out_im, out_re], axis=1))
    hi, lo = split2(jnp.concatenate(rows, axis=0))
    loads[4].wait()
    snd_b[...] = nt(cxt[0], hi) + nt(cxt[1], hi) + nt(cxt[0], lo)
    b_args = (snd_b, rcv_b, b_send, b_recv)
    exchange_rows(*b_args)

    stage(ua, ub, 0.5 * DT, DT / 3, 2, 9, False, 1, 2)
    stage(ub, ua, DT, DT / 3, 2, 9, False, 2, 1)
    stage(ua, None, DT, DT / 6, 4, 8, False, 1, None)

    after = []
    for p in range(4):
        parts = []
        for h in range(2):
            where = pl.ds(32 + 2 * p + h, 32, stride=8)
            cols = slice(128 * h, 128 * h + 128)
            u = [acc[f, where, :] for f in range(5)]
            for f in range(5):
                new_state[f, p, :, cols] = u[f]
            inv_rho = 1.0 / u[0]
            parts.append([u[1 + c] * inv_rho for c in range(3)])
        for c in range(3):
            after.append(jnp.concatenate([parts[0][c], parts[1][c]], axis=1))
    coarsen(jnp.concatenate(after, axis=0), snd_tg)
    tg_args = (lambda g: snd_tg.at[g], lambda g: rcv_tg.at[g], tg_send, tg_recv)
    start_across(*tg_args)
    rcv_tg[ga] = snd_tg[ga]

    wait_rows(*b_args)
    loads[5].wait()
    group = lax.broadcasted_iota(jnp.int32, (32, 128), 1) // 32
    for t in range(4):
        src = [rcv_b[pl.ds(4 * t + m, 32, stride=16), :] for m in range(4)]
        for j in range(4):
            made_of = None
            for m in range(4):
                turn = (32 * (m - j)) % 128
                piece = pltpu.roll(src[m], turn, 1) if turn else src[m]
                made_of = piece if made_of is None else jnp.where(group == m, piece, made_of)
            hi, lo = split2(made_of)
            rt_hi[pl.ds(32 * j, 32), 128 * t : 128 * t + 128] = hi
            rt_lo[pl.ds(32 * j, 32), 128 * t : 128 * t + 128] = lo

    lpx_hi, lpx_lo = split2(lpx_ref[...])
    k0, k1 = math.sqrt(2.0 / math.pi), 0.044715

    def transposed(a):
        a = jnp.concatenate([a, jnp.zeros((80, 128), F32)], axis=0)
        return a.T[:, :48]

    def forward(g, carry):
        at = pl.ds(pl.multiple_of(128 * g, 128), 128)
        ins_hi, ins_lo = split2(transposed(rcv_in[g]))
        pre = nn(inv[0, at, :], rt_hi[...]) + nn(inv[1, at, :], rt_hi[...]) + nn(inv[0, at, :], rt_lo[...])
        pre = pre + nn(ins_hi, lpx_hi) + nn(ins_hi, lpx_lo) + nn(ins_lo, lpx_hi)
        square = pre * pre
        t = jnp.tanh(k0 * pre * (1.0 + k1 * square))
        half = 0.5 * (1.0 + t)
        slope[at, :] = half + (0.5 * k0) * pre * (1.0 - t * t) * (1.0 + (3.0 * k1) * square)
        hi, lo = split2(pre * half)
        made[at, :] = nt(hi, pxt_ref[...]) + nt(lo, pxt_ref[...])
        return carry

    lax.fori_loop(0, GA, forward, 0)

    wait_across(*tg_args)

    def backward(g, carry):
        at = pl.ds(pl.multiple_of(128 * g, 128), 128)
        hi, lo = split2(made[at, :] - transposed(rcv_tg[g]))
        d_pre = (nn(hi, pxt_ref[...]) + nn(lo, pxt_ref[...])) * slope[at, :]
        hi, lo = split2(d_pre)
        dp_hi[at, :] = hi
        dp_lo[at, :] = lo
        return carry

    lax.fori_loop(0, GA, backward, 0)
    loads[6].wait()
    for t in range(4):
        cols = slice(128 * t, 128 * t + 128)
        ft[t] = nn(fjd[0], dp_hi[:, cols]) + nn(fjd[1], dp_hi[:, cols]) + nn(fjd[0], dp_lo[:, cols])
    for t in range(4):
        src = [ft[t, pl.ds(32 * j, 32), :] for j in range(4)]
        for m in range(4):
            made_of = None
            for j in range(4):
                turn = (32 * (j - m)) % 128
                piece = pltpu.roll(src[j], turn, 1) if turn else src[j]
                made_of = piece if made_of is None else jnp.where(group == j, piece, made_of)
            snd_g[pl.ds(4 * t + m, 32, stride=16), :] = made_of
    g_args = (snd_g, rcv_g, g_send, g_recv)
    exchange_rows(*g_args)
    wait_rows(*g_args)

    hi, lo = split2(rcv_g[...])
    turned = nn(cx[0], hi) + nn(cx[1], hi) + nn(cx[0], lo)
    cosine, sine = turned[:128].T, turned[128:].T
    for ky in range(2):
        re, im = slice(64 * ky, 64 * ky + 32), slice(64 * ky + 32, 64 * ky + 64)
        grads[ga, ky, 0] = cosine[re] + sine[im]
        grads[ga, ky, 1] = cosine[im] - sine[re]
    grads_args = (lambda g: grads.at[ga], lambda g: grads.at[g], gm_send, gm_recv)
    start_across(*grads_args)
    wait_across(*modes_args)
    wait_across(*grads_args)
    for ky in range(2):
        factor = jnp.where(2 * dev + ky == 0, 1.0, 2.0).astype(F32) / (XC * YC)
        for c in range(3):
            out_re, out_im = 0.0, 0.0
            for b in range(GA):
                x_re = modes[b, 8 * ky + 2 * c : 8 * ky + 2 * c + 1, :]
                x_im = modes[b, 8 * ky + 2 * c + 1 : 8 * ky + 2 * c + 2, :]
                g_re, g_im = grads[b, ky, 0], grads[b, ky, 1]
                out_re = out_re + (x_re * g_re + x_im * g_im)
                out_im = out_im + (x_re * g_im - x_im * g_re)
            t_out[ky, 0, c] = out_re * factor
            t_out[ky, 1, c] = out_im * factor


def expand_kernel(lift_s, t_ref, out_ref):
    part = [t_ref[0, 0, c] for c in range(3)]
    for i in range(WIDTH):
        out_ref[0, 0, i] = lift_s[0, i] * part[0] + lift_s[1, i] * part[1] + lift_s[2, i] * part[2]


def per_device(consts, density, velocity, pressure, lift, spectral, pointwise, project):
    lift_f = lift.astype(F32)
    vmem = pl.BlockSpec(memory_space=pltpu.VMEM)
    smem = pl.BlockSpec(memory_space=pltpu.SMEM)
    hbm = pl.BlockSpec(memory_space=pl.ANY)
    V = pltpu.VMEM
    dma = pltpu.SemaphoreType.DMA
    field = V((5, 384, 128), F32)
    rows = V((512, 128), F32)
    coarse = V((GA, 48, 128), F32)
    scratch = [
        V((2, 2, WIDTH, WIDTH, 128), BF16), V((2, 128, 512), BF16), V((2, 128, 512), BF16), V((2, 512, 128), BF16),
        V((2, 256, 512), BF16), V((2, 512, 256), BF16), V((256, 128), BF16),
        field, field, field, field, field, V((3, 5, 8, 384), F32),
        V((2, 5, 8, 128), F32), V((2, 2, 5, 8, 128), F32), V((2, 5, 8, 128), F32), V((4, 5, 8, 128), F32),
        V((384, 128), F32), coarse, coarse, coarse, coarse, rows, rows, rows, rows, rows, rows,
        V((2, 2, 3, WIDTH, 128), F32), V((GA, 16, 128), F32), V((GA, 2, 2, WIDTH, 128), F32),
        V((128, 512), BF16), V((128, 512), BF16), V((512, 512), F32), V((512, 48), F32),
        V((512, 512), BF16), V((512, 512), BF16), V((4, 128, 128), F32), V((48, 512), F32), V((48, 512), BF16),
        dma((7,)), dma((10,)), dma((10,)), dma((GA,)), dma((GA,)), dma((GA,)), dma((GA,)),
        dma((DEV,)), dma((DEV,)), dma((DEV,)), dma((DEV,)), dma((DEV,)), dma((DEV,)),
        dma((GA,)), dma((GA,)), dma((GA,)), dma((GA,)),
    ]
    new_state, t = pl.pallas_call(
        kernel,
        out_shape=(
            jax.ShapeDtypeStruct((5, 4, 32, 256), F32),
            jax.ShapeDtypeStruct((2, 2, 3, WIDTH, 128), F32),
        ),
        in_specs=[smem] + [vmem] * 6 + [hbm] * 7,
        out_specs=(vmem, vmem),
        scratch_shapes=scratch,
        compiler_params=pltpu.CompilerParams(
            collective_id=0, has_side_effects=True, vmem_limit_bytes=44 * 1024 * 1024
        ),
    )(lift_f, density, velocity, pressure, lift, pointwise, project, spectral, *consts)
    grad = pl.pallas_call(
        expand_kernel,
        grid=(2, 2),
        out_shape=jax.ShapeDtypeStruct((2, 2, WIDTH, WIDTH, 128), F32),
        in_specs=[smem, pl.BlockSpec((1, 1, 3, WIDTH, 128), lambda a, b: (a, b, 0, 0, 0))],
        out_specs=pl.BlockSpec((1, 1, WIDTH, WIDTH, 128), lambda a, b: (a, b, 0, 0, 0)),
    )(lift_f, t)
    return new_state, grad


def solution(mesh):
    in_specs = (
        P(None, "dev", "ga"),
        P(None, None, "dev", "ga"),
        P(None, "dev", "ga"),
        P(),
        P("dev", None, None, None, None),
        P(),
        P(),
    )
    out_specs = (P(None, None, "dev", "ga"), P("dev", None, None, None, None))

    def whole(*args):
        consts = tables()
        return jax.shard_map(
            lambda *a: per_device(a[:6], *a[6:]),
            mesh=mesh, in_specs=(P(),) * 6 + in_specs, out_specs=out_specs, check_vma=False,
        )(*[jnp.asarray(c) for c in consts], *args)

    return whole
```

profile of v0, /device:TPU:1, one launch (start us, length us, event | category | flops | bytes accessed | tf_op | source)
XLA Modules:
  0.0 66.2 jit_solution(9402673961176460828)
XLA Ops:
  0.6 0.7 %convert_element_type.3.lift_s = f32[3,32]{1,0:T(4,128)S(1)} convert(bf16[3,32]{1,0:T(4,128)(2,1)} %lift.1) | non-fusion elementwise | flops 96 | bytes 576 | tf_op jit(solution)/shard_map/convert_element_type | solution.py:532
  1.3 0.0 copy-start.11
  1.3 0.8 %copy.15.project = bf16[32,3]{1,0:T(8,128)(2,1)S(1)} copy(bf16[32,3]{0,1:T(4,128)(2,1)} %param.19) | data formatting | bytes 384 | tf_op args[6]
  2.1 0.0 copy-start
  2.1 1.2 %copy-done = bf16[2,2,32,32,128]{4,3,2,1,0:T(8,128)(2,1)S(1)} copy-done((bf16[2,2,32,32,128]{4,3,2,1,0:T(8,128)(2,1)S(1)}, bf16[2,2,32,32,128]{4,3,2,1,0:T(8,128)(2,1)}, u32[]{:S(2)}) %copy-start) | copy-done | bytes 1048600
  3.3 0.0 copy-start.1
  3.3 1.0 %copy-done.1 = bf16[2,512,256]{2,1,0:T(8,128)(2,1)S(1)} copy-done((bf16[2,512,256]{2,1,0:T(8,128)(2,1)S(1)}, bf16[2,512,256]{2,1,0:T(8,128)(2,1)}, u32[]{:S(2)}) %copy-start.1) | copy-done | bytes 524312
  4.4 0.0 copy-start.2
  4.4 1.0 %copy-done.2 = bf16[2,256,512]{2,1,0:T(8,128)(2,1)S(1)} copy-done((bf16[2,256,512]{2,1,0:T(8,128)(2,1)S(1)}, bf16[2,256,512]{2,1,0:T(8,128)(2,1)}, u32[]{:S(2)}) %copy-start.2) | copy-done | bytes 524312
  5.4 0.0 copy-start.3
  5.4 1.0 %copy-done.3 = f32[3,4,32,256]{3,2,1,0:T(8,128)S(1)} copy-done((f32[3,4,32,256]{3,2,1,0:T(8,128)S(1)}, f32[3,4,32,256]{3,2,1,0:T(8,128)}, u32[]{:S(2)}) %copy-start.3) | copy-done | bytes 393240
  6.4 0.0 copy-start.4
  6.4 0.9 %copy-done.4 = bf16[2,512,128]{2,1,0:T(8,128)(2,1)S(1)} copy-done((bf16[2,512,128]{2,1,0:T(8,128)(2,1)S(1)}, bf16[2,512,128]{2,1,0:T(8,128)(2,1)}, u32[]{:S(2)}) %copy-start.4) | copy-done | bytes 262168
  7.3 0.0 copy-start.5
  7.4 0.9 %copy-done.5 = bf16[2,128,512]{2,1,0:T(8,128)(2,1)S(1)} copy-done((bf16[2,128,512]{2,1,0:T(8,128)(2,1)S(1)}, bf16[2,128,512]{2,1,0:T(8,128)(2,1)}, u32[]{:S(2)}) %copy-start.5) | copy-done | bytes 262168
  8.3 0.0 copy-start.6
  8.3 0.9 %copy-done.6 = bf16[2,128,512]{2,1,0:T(8,128)(2,1)S(1)} copy-done((bf16[2,128,512]{2,1,0:T(8,128)(2,1)S(1)}, bf16[2,128,512]{2,1,0:T(8,128)(2,1)}, u32[]{:S(2)}) %copy-start.6) | copy-done | bytes 262168
  9.2 0.0 copy-start.8
  9.3 0.9 %copy-done.8 = f32[4,32,256]{2,1,0:T(8,128)S(1)} copy-done((f32[4,32,256]{2,1,0:T(8,128)S(1)}, f32[4,32,256]{2,1,0:T(8,128)}, u32[]{:S(2)}) %copy-start.8) | copy-done | bytes 131096
  10.2 0.0 copy-start.9
  10.2 0.9 %copy-done.9 = f32[4,32,256]{2,1,0:T(8,128)S(1)} copy-done((f32[4,32,256]{2,1,0:T(8,128)S(1)}, f32[4,32,256]{2,1,0:T(8,128)}, u32[]{:S(2)}) %copy-start.9) | copy-done | bytes 131096
  11.1 0.0 copy-start.10
  11.1 0.8 %copy-done.10 = bf16[256,128]{1,0:T(8,128)(2,1)S(1)} copy-done((bf16[256,128]{1,0:T(8,128)(2,1)S(1)}, bf16[256,128]{1,0:T(8,128)(2,1)}, u32[]{:S(2)}) %copy-start.10) | copy-done | bytes 65560
  11.9 0.0 copy-start.12
  11.9 0.7 %copy-done.12 = bf16[32,32]{1,0:T(8,128)(2,1)S(1)} copy-done((bf16[32,32]{1,0:T(8,128)(2,1)S(1)}, bf16[32,32]{1,0:T(8,128)(2,1)}, u32[]{:S(2)}) %copy-start.12) | copy-done | bytes 2072
  12.6 0.0 copy-start.13
  12.6 0.7 %copy-done.13 = bf16[3,32]{1,0:T(4,128)(2,1)S(1)} copy-done((bf16[3,32]{1,0:T(4,128)(2,1)S(1)}, bf16[3,32]{1,0:T(4,128)(2,1)}, u32[]{:S(2)}) %copy-start.13) | copy-done | bytes 216
  13.3 48.0 %shard_map.140 = (f32[5,4,32,256]{3,2,1,0:T(8,128)S(1)}, f32[2,2,3,32,128]{4,3,2,1,0:T(8,128)S(1)}) custom-call(f32[3,32]{1,0:T(4,128)S(1)} %convert_element_type.3.lift_s, f32[4,32,256]{2,1,0:T(8,128)S(1)} %copy-done.8, f32[3,4,32,256]{3,2,1,0:T(8,128)S(1)} %copy-done.3, f32[4,32,256]{2,1,0:T(8,128)S(1)} %copy-done.9, bf16[3,32]{1,0:T(4,128)(2,1)S(1)} %copy-done.13, ...), custom_call_target="tpu_custom_call" | custom-call | tf_op jit(solution)/shard_map/pallas_call | solution.py:554
  61.2 0.0 copy-start.7
  61.3 0.7 %copy-done.7 = f32[2,2,3,32,128]{4,3,2,1,0:T(8,128)} copy-done((f32[2,2,3,32,128]{4,3,2,1,0:T(8,128)}, f32[2,2,3,32,128]{4,3,2,1,0:T(8,128)S(1)}, u32[]{:S(2)}) %copy-start.7) | copy-done | bytes 196632
  61.9 0.0 copy-done.11
  61.9 3.4 %shard_map.141 = f32[2,2,32,32,128]{4,3,2,1,0:T(8,128)} custom-call(f32[3,32]{1,0:T(4,128)} %copy-done.11, f32[2,2,3,32,128]{4,3,2,1,0:T(8,128)} %copy-done.7), custom_call_target="tpu_custom_call" | custom-call | tf_op jit(solution)/shard_map/pallas_call | solution.py:567
  65.4 0.8 %copy.17 = f32[5,4,32,256]{3,2,1,0:T(8,128)} copy(f32[5,4,32,256]{3,2,1,0:T(8,128)S(1)} %get-tuple-element.8) | data formatting | bytes 1310720
Async XLA Ops:
  1.3 60.6 %copy-start.11 = (f32[3,32]{1,0:T(4,128)}, f32[3,32]{1,0:T(4,128)S(1)}, u32[]{:S(2)}) copy-start(f32[3,32]{1,0:T(4,128)S(1)} %convert_element_type.3.lift_s) | copy-start | bytes 1156
  2.1 1.2 %copy-start = (bf16[2,2,32,32,128]{4,3,2,1,0:T(8,128)(2,1)S(1)}, bf16[2,2,32,32,128]{4,3,2,1,0:T(8,128)(2,1)}, u32[]{:S(2)}) copy-start(bf16[2,2,32,32,128]{4,3,2,1,0:T(8,128)(2,1)} %spectral_h.1) | copy-start | bytes 3145732
  3.3 1.0 %copy-start.1 = (bf16[2,512,256]{2,1,0:T(8,128)(2,1)S(1)}, bf16[2,512,256]{2,1,0:T(8,128)(2,1)}, u32[]{:S(2)}) copy-start(bf16[2,512,256]{2,1,0:T(8,128)(2,1)} %constant.16.clone.cxt_h) | copy-start | bytes 1572868
  4.4 1.0 %copy-start.2 = (bf16[2,256,512]{2,1,0:T(8,128)(2,1)S(1)}, bf16[2,256,512]{2,1,0:T(8,128)(2,1)}, u32[]{:S(2)}) copy-start(bf16[2,256,512]{2,1,0:T(8,128)(2,1)} %constant.15.clone.cx_h) | copy-start | bytes 1572868
  5.4 1.0 %copy-start.3 = (f32[3,4,32,256]{3,2,1,0:T(8,128)S(1)}, f32[3,4,32,256]{3,2,1,0:T(8,128)}, u32[]{:S(2)}) copy-start(f32[3,4,32,256]{3,2,1,0:T(8,128)} %velocity.1) | copy-start | bytes 1179652
  6.4 0.9 %copy-start.4 = (bf16[2,512,128]{2,1,0:T(8,128)(2,1)S(1)}, bf16[2,512,128]{2,1,0:T(8,128)(2,1)}, u32[]{:S(2)}) copy-start(bf16[2,512,128]{2,1,0:T(8,128)(2,1)} %constant.14.clone.inv_h) | copy-start | bytes 786436
  7.3 0.9 %copy-start.5 = (bf16[2,128,512]{2,1,0:T(8,128)(2,1)S(1)}, bf16[2,128,512]{2,1,0:T(8,128)(2,1)}, u32[]{:S(2)}) copy-start(bf16[2,128,512]{2,1,0:T(8,128)(2,1)} %constant.13.clone.fjd_h) | copy-start | bytes 786436
  8.3 0.9 %copy-start.6 = (bf16[2,128,512]{2,1,0:T(8,128)(2,1)S(1)}, bf16[2,128,512]{2,1,0:T(8,128)(2,1)}, u32[]{:S(2)}) copy-start(bf16[2,128,512]{2,1,0:T(8,128)(2,1)} %constant.12.clone.fdj_h) | copy-start | bytes 786436
  9.2 0.9 %copy-start.8 = (f32[4,32,256]{2,1,0:T(8,128)S(1)}, f32[4,32,256]{2,1,0:T(8,128)}, u32[]{:S(2)}) copy-start(f32[4,32,256]{2,1,0:T(8,128)} %density.1) | copy-start | bytes 393220
  10.2 0.9 %copy-start.9 = (f32[4,32,256]{2,1,0:T(8,128)S(1)}, f32[4,32,256]{2,1,0:T(8,128)}, u32[]{:S(2)}) copy-start(f32[4,32,256]{2,1,0:T(8,128)} %pressure.1) | copy-start | bytes 393220
  11.1 0.8 %copy-start.10 = (bf16[256,128]{1,0:T(8,128)(2,1)S(1)}, bf16[256,128]{1,0:T(8,128)(2,1)}, u32[]{:S(2)}) copy-start(bf16[256,128]{1,0:T(8,128)(2,1)} %constant.17.clone.pool_h) | copy-start | bytes 196612
  11.9 0.7 %copy-start.12 = (bf16[32,32]{1,0:T(8,128)(2,1)S(1)}, bf16[32,32]{1,0:T(8,128)(2,1)}, u32[]{:S(2)}) copy-start(bf16[32,32]{1,0:T(8,128)(2,1)} %pointwise.1) | copy-start | bytes 6148
  12.6 0.7 %copy-start.13 = (bf16[3,32]{1,0:T(4,128)(2,1)S(1)}, bf16[3,32]{1,0:T(4,128)(2,1)}, u32[]{:S(2)}) copy-start(bf16[3,32]{1,0:T(4,128)(2,1)} %lift.1) | copy-start | bytes 580
  61.2 0.7 %copy-start.7 = (f32[2,2,3,32,128]{4,3,2,1,0:T(8,128)}, f32[2,2,3,32,128]{4,3,2,1,0:T(8,128)S(1)}, u32[]{:S(2)}) copy-start(f32[2,2,3,32,128]{4,3,2,1,0:T(8,128)S(1)} %get-tuple-element.5.t_ref) | copy-start | bytes 589828
where the time goes:
time: 66.9 us; the launch traced here: 66.2 us
  Pallas kernels  51.4 us (77%)
  local copies, waits for them, and re-layouts  13.5 us (20%)
  other arithmetic  0.68 us (1%)
    pallas_call x1, Pallas kernels, per_device(): pl.pallas_call(kernel, out_shape=(jax.ShapeDtypeStruct((5, 4, 32, 256), F...  48 us
    unnamed x30, local copies, waits for them, and re-layouts  13.5 us
    pallas_call x1, Pallas kernels, per_device(): pl.pallas_call(expand_kernel, grid=(2, 2), out_shape=jax.ShapeDtypeStruct...  3.42 us

commit v1 on v0

--- a/solution.py
+++ b/solution.py
@@ -19,6 +19,7 @@
 GA = 4
 DEV = 32
 DT = 0.12
+VMEM_BYTES = 62 * 1024 * 1024
 
 
 def tables():
@@ -93,6 +94,11 @@
 def faces(ul, ur, fl, fr, sl, sr):
     top = jnp.maximum(sl, sr)
     return [(a + b) - top * (d - c) for a, b, c, d in zip(fl, fr, ul, ur)]
+
+
+def widened(lift, c):
+    pick = (lax.broadcasted_iota(jnp.int32, (3, 128), 0) == c).astype(F32).astype(BF16)
+    return tn(lift, pick)
 
 
 def rim_rates(u):
@@ -153,9 +159,10 @@
 
 
 def kernel(
-    lift_s, density, velocity, pressure, lift, pointwise, project, spectral_h,
+    density_h, velocity_h, pressure_h, lift_h, pointwise_h, project_h, spectral_h,
     fdj_h, fjd_h, inv_h, cx_h, cxt_h, pool_h,
-    new_state, t_out,
+    new_state_h, t_out,
+    density, velocity, pressure, lift, pointwise, project, new_state, lift_wide,
     spectral, fdj, fjd, inv, cx, cxt, pool,
     u0, ua, ub, acc, edge, rim, own_edge, side_edge, row_edge, corner_edge,
     pooled, snd_in, rcv_in, snd_tg, rcv_tg, snd_x, rcv_x, snd_b, rcv_b, snd_g, rcv_g,
@@ -171,11 +178,15 @@
     loads = [
         pltpu.make_async_copy(a, b, load_sem.at[n])
         for n, (a, b) in enumerate(
-            ((pool_h, pool), (spectral_h, spectral), (fdj_h, fdj), (cx_h, cx), (cxt_h, cxt), (inv_h, inv), (fjd_h, fjd))
+            (
+                (pool_h, pool), (spectral_h, spectral), (fdj_h, fdj), (cx_h, cx), (cxt_h, cxt), (inv_h, inv), (fjd_h, fjd),
+                (density_h, density), (velocity_h, velocity), (pressure_h, pressure),
+                (lift_h, lift), (pointwise_h, pointwise), (project_h, project),
+            )
         )
     ]
-    for c in loads:
-        c.start()
+    for n in (7, 8, 9, 0, 10, 11, 12, 1, 2, 3, 4, 5, 6):
+        loads[n].start()
 
     barrier = pltpu.get_barrier_semaphore()
 
@@ -238,6 +249,8 @@
         both = pooled[pl.ds(0, 192, stride=2), :] + pooled[pl.ds(1, 192, stride=2), :]
         snd[...] = both.reshape(GA, 48, 128)
 
+    for n in (7, 8, 9):
+        loads[n].wait()
     for p in range(4):
         for h in range(2):
             cols = slice(128 * h, 128 * h + 128)
@@ -287,7 +300,10 @@
         c.start()
     rcv_in[ga] = snd_in[ga]
 
-    loads[1].wait()
+    for n in (10, 11, 12, 1):
+        loads[n].wait()
+    for c in range(3):
+        lift_wide[c] = widened(lift[...], c)
     for ky in range(2):
         for part in range(2):
 
@@ -297,7 +313,7 @@
                     w = 4 * w8 + n
                     s = spectral[ky, part, w].astype(F32)
                     for c in range(3):
-                        total[c] = total[c] + lift_s[c, w] * s
+                        total[c] = total[c] + jnp.broadcast_to(lift_wide[c, pl.ds(w, 1), :], (WIDTH, 128)) * s
                 return tuple(total)
 
             zero = jnp.zeros((WIDTH, 128), F32)
@@ -319,7 +335,7 @@
 
     lp_hi, lp_lo = split2(nn(lift[...], pointwise[...]))
     lpx_ref[...] = spread(nn(lp_hi, tile_o) + nn(lp_lo, tile_o))
-    pxt_ref[...] = spread(tn(project[...], tile_o)).astype(BF16)
+    pxt_ref[...] = spread(nn(project[...], tile_o)).astype(BF16)
 
     wait_across(*in_args)
     loads[2].wait()
@@ -427,6 +443,8 @@
         for c in range(3):
             after.append(jnp.concatenate([parts[0][c], parts[1][c]], axis=1))
     coarsen(jnp.concatenate(after, axis=0), snd_tg)
+    state_copy = pltpu.make_async_copy(new_state, new_state_h, load_sem.at[13])
+    state_copy.start()
     tg_args = (lambda g: snd_tg.at[g], lambda g: rcv_tg.at[g], tg_send, tg_recv)
     start_across(*tg_args)
     rcv_tg[ga] = snd_tg[ga]
@@ -520,18 +538,52 @@
                 out_im = out_im + (x_re * g_im - x_im * g_re)
             t_out[ky, 0, c] = out_re * factor
             t_out[ky, 1, c] = out_im * factor
-
-
-def expand_kernel(lift_s, t_ref, out_ref):
-    part = [t_ref[0, 0, c] for c in range(3)]
-    for i in range(WIDTH):
-        out_ref[0, 0, i] = lift_s[0, i] * part[0] + lift_s[1, i] * part[1] + lift_s[2, i] * part[2]
+    state_copy.wait()
+
+
+def expand_kernel(lift_h, t_h, state_h, out_h, new_state_h, lift, t, state, lift_wide, out, sem):
+    loads = [
+        pltpu.make_async_copy(a, b, sem.at[n]) for n, (a, b) in enumerate(((lift_h, lift), (t_h, t), (state_h, state)))
+    ]
+    for c in loads:
+        c.start()
+    forward = pltpu.make_async_copy(state, new_state_h, sem.at[19])
+    loads[0].wait()
+    for c in range(3):
+        lift_wide[c] = widened(lift[...], c)
+    loads[1].wait()
+
+    def stretch(n):
+        ky, rest = n // 8, n % 8
+        part, rows = rest // 4, pl.ds(8 * (rest % 4), 8)
+        return pltpu.make_async_copy(out.at[ky, part, rows], out_h.at[ky, part, rows], sem.at[3 + n])
+
+    def body(n, carry):
+        ky, rest = n // 8, n % 8
+        part, first = rest // 4, 8 * (rest % 4)
+        terms = [t[ky, part, c] for c in range(3)]
+        for i in range(8):
+            total = 0.0
+            for c in range(3):
+                total = total + jnp.broadcast_to(lift_wide[c, pl.ds(first + i, 1), :], (WIDTH, 128)) * terms[c]
+            out[ky, part, first + i] = total
+        stretch(n).start()
+        return carry
+
+    lax.fori_loop(0, 4, body, 0)
+    loads[2].wait()
+    forward.start()
+    lax.fori_loop(4, 16, body, 0)
+
+    def done(n, carry):
+        stretch(n).wait()
+        return carry
+
+    lax.fori_loop(0, 16, done, 0)
+    forward.wait()
 
 
 def per_device(consts, density, velocity, pressure, lift, spectral, pointwise, project):
-    lift_f = lift.astype(F32)
-    vmem = pl.BlockSpec(memory_space=pltpu.VMEM)
-    smem = pl.BlockSpec(memory_space=pltpu.SMEM)
     hbm = pl.BlockSpec(memory_space=pl.ANY)
     V = pltpu.VMEM
     dma = pltpu.SemaphoreType.DMA
@@ -539,6 +591,8 @@
     rows = V((512, 128), F32)
     coarse = V((GA, 48, 128), F32)
     scratch = [
+        V((4, 32, 256), F32), V((3, 4, 32, 256), F32), V((4, 32, 256), F32), V((3, WIDTH), BF16), V((WIDTH, WIDTH), BF16),
+        V((3, WIDTH), BF16), V((5, 4, 32, 256), F32), V((3, WIDTH, 128), F32),
         V((2, 2, WIDTH, WIDTH, 128), BF16), V((2, 128, 512), BF16), V((2, 128, 512), BF16), V((2, 512, 128), BF16),
         V((2, 256, 512), BF16), V((2, 512, 256), BF16), V((256, 128), BF16),
         field, field, field, field, field, V((3, 5, 8, 384), F32),
@@ -547,7 +601,7 @@
         V((2, 2, 3, WIDTH, 128), F32), V((GA, 16, 128), F32), V((GA, 2, 2, WIDTH, 128), F32),
         V((128, 512), BF16), V((128, 512), BF16), V((512, 512), F32), V((512, 48), F32),
         V((512, 512), BF16), V((512, 512), BF16), V((4, 128, 128), F32), V((48, 512), F32), V((48, 512), BF16),
-        dma((7,)), dma((10,)), dma((10,)), dma((GA,)), dma((GA,)), dma((GA,)), dma((GA,)),
+        dma((14,)), dma((10,)), dma((10,)), dma((GA,)), dma((GA,)), dma((GA,)), dma((GA,)),
         dma((DEV,)), dma((DEV,)), dma((DEV,)), dma((DEV,)), dma((DEV,)), dma((DEV,)),
         dma((GA,)), dma((GA,)), dma((GA,)), dma((GA,)),
     ]
@@ -557,20 +611,27 @@
             jax.ShapeDtypeStruct((5, 4, 32, 256), F32),
             jax.ShapeDtypeStruct((2, 2, 3, WIDTH, 128), F32),
         ),
-        in_specs=[smem] + [vmem] * 6 + [hbm] * 7,
-        out_specs=(vmem, vmem),
+        in_specs=[hbm] * 13,
+        out_specs=(hbm, pl.BlockSpec(memory_space=pltpu.VMEM)),
         scratch_shapes=scratch,
         compiler_params=pltpu.CompilerParams(
-            collective_id=0, has_side_effects=True, vmem_limit_bytes=44 * 1024 * 1024
+            collective_id=0, has_side_effects=True, vmem_limit_bytes=VMEM_BYTES
         ),
-    )(lift_f, density, velocity, pressure, lift, pointwise, project, spectral, *consts)
-    grad = pl.pallas_call(
+    )(density, velocity, pressure, lift, pointwise, project.T, spectral, *consts)
+    grad, new_state = pl.pallas_call(
         expand_kernel,
-        grid=(2, 2),
-        out_shape=jax.ShapeDtypeStruct((2, 2, WIDTH, WIDTH, 128), F32),
-        in_specs=[smem, pl.BlockSpec((1, 1, 3, WIDTH, 128), lambda a, b: (a, b, 0, 0, 0))],
-        out_specs=pl.BlockSpec((1, 1, WIDTH, WIDTH, 128), lambda a, b: (a, b, 0, 0, 0)),
-    )(lift_f, t)
+        out_shape=(
+            jax.ShapeDtypeStruct((2, 2, WIDTH, WIDTH, 128), F32),
+            jax.ShapeDtypeStruct((5, 4, 32, 256), F32),
+        ),
+        in_specs=[hbm] * 3,
+        out_specs=(hbm, hbm),
+        scratch_shapes=[
+            V((3, WIDTH), BF16), V((2, 2, 3, WIDTH, 128), F32), V((5, 4, 32, 256), F32), V((3, WIDTH, 128), F32),
+            V((2, 2, WIDTH, WIDTH, 128), F32), dma((20,)),
+        ],
+        compiler_params=pltpu.CompilerParams(vmem_limit_bytes=VMEM_BYTES),
+    )(lift, t, new_state)
     return new_state, grad
 
 

time: 66.9 us -> 51.6 us (0.77)
  local copies, waits for them, and re-layouts: 13.5 us -> 0 us
  other arithmetic: 0.68 us -> 0 us
    unnamed x30 -> x0, local copies, waits for them, and re-layouts: 13.5 us -> none
    pallas_call x1, Pallas kernels: 3.42 us -> 2.73 us  [per_device(): pl.pallas_call(expand_kernel, out_shape=(jax.ShapeDtypeStruct((2, 2, WIDT...]
    convert_element_type x1 -> x0, other arithmetic: 0.68 us -> none  [per_device(): lift_f = lift.astype(F32)]
where the time goes in v1:
time: 51.6 us; the launch traced here: 51.4 us
  Pallas kernels  50.8 us (98%)
  between operations  0.64 us (1%)
    pallas_call x1, Pallas kernels, per_device(): pl.pallas_call(kernel, out_shape=(jax.ShapeDtypeStruct((5, 4, 32, 256), F...  48.1 us
    pallas_call x1, Pallas kernels, per_device(): pl.pallas_call(expand_kernel, out_shape=(jax.ShapeDtypeStruct((2, 2, WIDT...  2.73 us

profile of v1, /device:TPU:1, one launch (start us, length us, event | category | flops | bytes accessed | tf_op | source)
XLA Modules:
  0.0 51.4 jit_solution(4571103412710280504)
XLA Ops:
  0.6 48.1 %shard_map.140 = (f32[5,4,32,256]{3,2,1,0:T(8,128)}, f32[2,2,3,32,128]{4,3,2,1,0:T(8,128)}) custom-call(f32[4,32,256]{2,1,0:T(8,128)} %density_h.1, f32[3,4,32,256]{3,2,1,0:T(8,128)} %velocity_h.1, f32[4,32,256]{2,1,0:T(8,128)} %pressure_h.1, bf16[3,32]{1,0:T(4,128)(2,1)} %lift_h.3, bf16[32,32]{1,0:T(8,128)(2,1)} %pointwise_h.1, bf16[3,32]{1,0:T(4,128)(2,1)} %bitcast.1, ...), custom_call_target="tpu_custom_call" | custom-call | tf_op jit(solution)/shard_map/pallas_call | solution.py:608
  48.7 2.7 %shard_map.141 = (f32[2,2,32,32,128]{4,3,2,1,0:T(8,128)}, f32[5,4,32,256]{3,2,1,0:T(8,128)}) custom-call(bf16[3,32]{1,0:T(4,128)(2,1)} %lift_h.3, f32[2,2,3,32,128]{4,3,2,1,0:T(8,128)} %get-tuple-element.6.t_h, f32[5,4,32,256]{3,2,1,0:T(8,128)} %get-tuple-element.7.state_h), custom_call_target="tpu_custom_call" | custom-call | tf_op jit(solution)/shard_map/pallas_call | solution.py:621

commit v2 on v1

--- a/solution.py
+++ b/solution.py
@@ -19,10 +19,20 @@
 GA = 4
 DEV = 32
 DT = 0.12
+OFFSETS = sorted(
+    ((a, b, c) for a in range(4) for b in range(4) for c in range(2) if a + b + c),
+    key=lambda o: (-min(o[0], 4 - o[0]) - min(o[1], 4 - o[1]), o),
+)
 VMEM_BYTES = 62 * 1024 * 1024
 
 
 def tables():
+    def split(a):
+        a = np.asarray(a, np.float32)
+        hi = a.astype(jnp.bfloat16)
+        lo = (a - hi.astype(np.float32)).astype(jnp.bfloat16)
+        return np.ascontiguousarray(np.stack([hi, lo]))
+
     ky = np.arange(MODES)
     y = np.arange(YC)
     ang = 2 * np.pi * ((ky[:, None] * y[None, :]) % YC) / YC
@@ -36,20 +46,16 @@
     kx = np.where(q < MODES, q, XC - 2 * MODES + q)
     ax = 2 * np.pi * ((kx[:, None] * np.arange(XC)[None, :]) % XC) / XC
     cx = np.concatenate([np.cos(ax), np.sin(ax)], axis=0)
-
-    def split(a):
-        a = np.asarray(a, np.float32)
-        hi = a.astype(jnp.bfloat16)
-        lo = (a - hi.astype(np.float32)).astype(jnp.bfloat16)
-        return np.ascontiguousarray(np.stack([hi, lo]))
+    cx_halves = cx.reshape(256, DEV, 2, 8).transpose(0, 2, 1, 3).reshape(256, XC)
+    inv_hi, inv_lo = split(inv_jd)
 
     pool = np.zeros((256, 128), np.float32)
     pool[np.arange(256), np.arange(256) // 2] = 0.25
     return (
         split(fwd_dj.reshape(128, YC)),
         split(fwd_jd),
-        split(inv_jd),
-        split(cx),
+        np.concatenate([inv_hi, inv_hi, inv_lo], axis=1),
+        split(cx_halves),
         split(cx.T),
         pool.astype(jnp.bfloat16),
     )
@@ -166,7 +172,7 @@
     spectral, fdj, fjd, inv, cx, cxt, pool,
     u0, ua, ub, acc, edge, rim, own_edge, side_edge, row_edge, corner_edge,
     pooled, snd_in, rcv_in, snd_tg, rcv_tg, snd_x, rcv_x, snd_b, rcv_b, snd_g, rcv_g,
-    contracted, modes, grads, rt_hi, rt_lo, slope, made, dp_hi, dp_lo, ft, lpx_ref, pxt_ref,
+    contracted, modes, grads, rt, slope, made, dp_hi, dp_lo, ft, lpx_ref, pxt_ref,
     load_sem, halo_send, halo_recv, in_send, in_recv, tg_send, tg_recv, x_send, x_recv, b_send, b_recv,
     g_send, g_recv, xm_send, xm_recv, gm_send, gm_recv,
 ):
@@ -201,25 +207,24 @@
         for b in (south, north):
             pl.semaphore_signal(barrier, inc=1, device_id=(a, b), device_id_type=MESH)
 
-    def exchange_rows(snd, rcv, ssem, rsem):
-        def go(s, carry):
-            peer = lax.rem(dev + s, DEV)
+    core, chip_x, chip_y = lax.rem(dev, 2), lax.rem(lax.div(dev, 2), 4), lax.div(dev, 8)
+
+    def exchange_rows(snd, rcv, ssem, rsem, unit):
+        for dy, dx, dc in OFFSETS:
+            peer = lax.rem(chip_y + dy, 4) * 8 + lax.rem(chip_x + dx, 4) * 2 + lax.rem(core + dc, 2)
             pltpu.make_async_remote_copy(
-                src_ref=snd.at[pl.ds(pl.multiple_of(16 * peer, 16), 16)],
-                dst_ref=rcv.at[pl.ds(pl.multiple_of(16 * dev, 16), 16)],
+                src_ref=snd.at[pl.ds(pl.multiple_of(unit * peer, unit), unit)],
+                dst_ref=rcv.at[pl.ds(pl.multiple_of(unit * dev, unit), unit)],
                 send_sem=ssem.at[peer], recv_sem=rsem.at[dev],
                 device_id=(ga, peer), device_id_type=MESH,
             ).start()
-            return carry
-
-        lax.fori_loop(1, DEV, go, 0)
-        mine = pl.ds(pl.multiple_of(16 * dev, 16), 16)
+        mine = pl.ds(pl.multiple_of(unit * dev, unit), unit)
         rcv[mine, :] = snd[mine, :]
 
-    def wait_rows(snd, rcv, ssem, rsem):
+    def wait_rows(snd, rcv, ssem, rsem, unit):
         def go(s, carry):
             peer = lax.rem(dev + s, DEV)
-            at = pl.ds(pl.multiple_of(16 * peer, 16), 16)
+            at = pl.ds(pl.multiple_of(unit * peer, unit), unit)
             pltpu.make_async_remote_copy(
                 src_ref=snd.at[at], dst_ref=rcv.at[at], send_sem=ssem.at[peer], recv_sem=rsem.at[peer],
                 device_id=(ga, peer), device_id_type=MESH,
@@ -236,11 +241,11 @@
         )
 
     def start_across(src, dst, ssem, rsem):
-        for s in (1, 3, 2):
+        for s in (2, 1, 3):
             across(s, src, dst, ssem, rsem, False).start()
 
     def wait_across(src, dst, ssem, rsem):
-        for s in (1, 3, 2):
+        for s in (2, 1, 3):
             across(s, src, dst, ssem, rsem, True).wait()
 
     def coarsen(rows, snd):
@@ -335,17 +340,21 @@
 
     lp_hi, lp_lo = split2(nn(lift[...], pointwise[...]))
     lpx_ref[...] = spread(nn(lp_hi, tile_o) + nn(lp_lo, tile_o))
-    pxt_ref[...] = spread(nn(project[...], tile_o)).astype(BF16)
+    spread_out = jnp.concatenate([spread(nn(project[...], tile_o)), jnp.zeros((80, 512), F32)], axis=0)
+    pxt_ref[...] = jnp.concatenate([spread_out, spread_out], axis=0).astype(BF16)
 
     wait_across(*in_args)
     loads[2].wait()
     hi, lo = split2(jnp.concatenate([rcv_in[g] for g in range(GA)], axis=1))
     freq = nt(hi, fdj[0]) + nt(hi, fdj[1]) + nt(lo, fdj[0])
-    lane2 = lax.broadcasted_iota(jnp.int32, (16, 128), 1)
     for d in range(DEV):
-        a, b, c = (pltpu.roll(freq[16 * n : 16 * n + 16], (4 * n - 4 * d) % 128, 1) for n in range(3))
-        snd_x[pl.ds(16 * d, 16), :] = jnp.where(lane2 < 4, a, jnp.where(lane2 < 8, b, c))
-    x_args = (snd_x, rcv_x, x_send, x_recv)
+        packed = None
+        for n in range(6):
+            h, c = n // 3, n % 3
+            piece = pltpu.roll(freq[16 * c + 8 * h : 16 * c + 8 * h + 8], (16 * h + 4 * c - 4 * d) % 128, 1)
+            packed = piece if packed is None else jnp.where(lane1 >= 16 * h + 4 * c, piece, packed)
+        snd_x[pl.ds(8 * d, 8), :] = packed
+    x_args = (snd_x, rcv_x, x_send, x_recv, 8)
     exchange_rows(*x_args)
 
     for c in halos:
@@ -393,11 +402,16 @@
         lax.fori_loop(0, blocks, block, 0)
 
     stage(u0, ua, 0.5 * DT, DT / 6, 1, 10, True, 0, 1)
+    stage(ua, ub, 0.5 * DT, DT / 3, 2, 9, False, 1, 2)
 
     wait_rows(*x_args)
     loads[3].wait()
     hi, lo = split2(rcv_x[...])
-    turned = nn(cx[0], hi) + nn(cx[1], hi) + nn(cx[0], lo)
+    turned = 0.0
+    for h in range(2):
+        cols = slice(256 * h, 256 * h + 256)
+        half = nn(cx[0, :, cols], hi) + nn(cx[1, :, cols], hi) + nn(cx[0, :, cols], lo)
+        turned = turned + (pltpu.roll(half, 112, 1) if h else half)
     cosine, sine = turned[:128].T, turned[128:].T
     for ky in range(2):
         for c in range(3):
@@ -422,10 +436,9 @@
     hi, lo = split2(jnp.concatenate(rows, axis=0))
     loads[4].wait()
     snd_b[...] = nt(cxt[0], hi) + nt(cxt[1], hi) + nt(cxt[0], lo)
-    b_args = (snd_b, rcv_b, b_send, b_recv)
+    b_args = (snd_b, rcv_b, b_send, b_recv, 16)
     exchange_rows(*b_args)
 
-    stage(ua, ub, 0.5 * DT, DT / 3, 2, 9, False, 1, 2)
     stage(ub, ua, DT, DT / 3, 2, 9, False, 2, 1)
     stage(ua, None, DT, DT / 6, 4, 8, False, 1, None)
 
@@ -449,6 +462,15 @@
     start_across(*tg_args)
     rcv_tg[ga] = snd_tg[ga]
 
+    lpx_hi, lpx_lo = split2(lpx_ref[...])
+
+    def transposed(a):
+        return jnp.concatenate([a, jnp.zeros((80, 128), F32)], axis=0).T
+
+    for g in range(GA):
+        ins_hi, ins_lo = split2(transposed(rcv_in[g])[:, :48])
+        slope[pl.ds(128 * g, 128), :] = nn(ins_hi, lpx_hi) + nn(ins_hi, lpx_lo) + nn(ins_lo, lpx_hi)
+
     wait_rows(*b_args)
     loads[5].wait()
     group = lax.broadcasted_iota(jnp.int32, (32, 128), 1) // 32
@@ -461,27 +483,20 @@
                 piece = pltpu.roll(src[m], turn, 1) if turn else src[m]
                 made_of = piece if made_of is None else jnp.where(group == m, piece, made_of)
             hi, lo = split2(made_of)
-            rt_hi[pl.ds(32 * j, 32), 128 * t : 128 * t + 128] = hi
-            rt_lo[pl.ds(32 * j, 32), 128 * t : 128 * t + 128] = lo
-
-    lpx_hi, lpx_lo = split2(lpx_ref[...])
+            for n, piece in enumerate((hi, lo, hi)):
+                rt[pl.ds(128 * n + 32 * j, 32), 128 * t : 128 * t + 128] = piece
+
     k0, k1 = math.sqrt(2.0 / math.pi), 0.044715
-
-    def transposed(a):
-        a = jnp.concatenate([a, jnp.zeros((80, 128), F32)], axis=0)
-        return a.T[:, :48]
 
     def forward(g, carry):
         at = pl.ds(pl.multiple_of(128 * g, 128), 128)
-        ins_hi, ins_lo = split2(transposed(rcv_in[g]))
-        pre = nn(inv[0, at, :], rt_hi[...]) + nn(inv[1, at, :], rt_hi[...]) + nn(inv[0, at, :], rt_lo[...])
-        pre = pre + nn(ins_hi, lpx_hi) + nn(ins_hi, lpx_lo) + nn(ins_lo, lpx_hi)
+        pre = slope[at, :] + nn(inv[at, :], rt[...])
         square = pre * pre
         t = jnp.tanh(k0 * pre * (1.0 + k1 * square))
         half = 0.5 * (1.0 + t)
         slope[at, :] = half + (0.5 * k0) * pre * (1.0 - t * t) * (1.0 + (3.0 * k1) * square)
         hi, lo = split2(pre * half)
-        made[at, :] = nt(hi, pxt_ref[...]) + nt(lo, pxt_ref[...])
+        made[at, :] = nt(hi, pxt_ref[:128]) + nt(lo, pxt_ref[:128])
         return carry
 
     lax.fori_loop(0, GA, forward, 0)
@@ -491,7 +506,7 @@
     def backward(g, carry):
         at = pl.ds(pl.multiple_of(128 * g, 128), 128)
         hi, lo = split2(made[at, :] - transposed(rcv_tg[g]))
-        d_pre = (nn(hi, pxt_ref[...]) + nn(lo, pxt_ref[...])) * slope[at, :]
+        d_pre = nn(jnp.concatenate([hi, lo], axis=1), pxt_ref[...]) * slope[at, :]
         hi, lo = split2(d_pre)
         dp_hi[at, :] = hi
         dp_lo[at, :] = lo
@@ -499,9 +514,10 @@
 
     lax.fori_loop(0, GA, backward, 0)
     loads[6].wait()
-    for t in range(4):
-        cols = slice(128 * t, 128 * t + 128)
-        ft[t] = nn(fjd[0], dp_hi[:, cols]) + nn(fjd[1], dp_hi[:, cols]) + nn(fjd[0], dp_lo[:, cols])
+    for t in range(2):
+        cols = slice(256 * t, 256 * t + 256)
+        both = nn(fjd[0], dp_hi[:, cols]) + nn(fjd[1], dp_hi[:, cols]) + nn(fjd[0], dp_lo[:, cols])
+        ft[2 * t], ft[2 * t + 1] = both[:, :128], both[:, 128:]
     for t in range(4):
         src = [ft[t, pl.ds(32 * j, 32), :] for j in range(4)]
         for m in range(4):
@@ -511,11 +527,12 @@
                 piece = pltpu.roll(src[j], turn, 1) if turn else src[j]
                 made_of = piece if made_of is None else jnp.where(group == j, piece, made_of)
             snd_g[pl.ds(4 * t + m, 32, stride=16), :] = made_of
-    g_args = (snd_g, rcv_g, g_send, g_recv)
+    g_args = (snd_g, rcv_g, g_send, g_recv, 16)
     exchange_rows(*g_args)
     wait_rows(*g_args)
 
-    hi, lo = split2(rcv_g[...])
+    arrived = rcv_g[...].reshape(DEV, 2, 8, 128)
+    hi, lo = split2(jnp.concatenate([arrived[:, h].reshape(256, 128) for h in range(2)], axis=0))
     turned = nn(cx[0], hi) + nn(cx[1], hi) + nn(cx[0], lo)
     cosine, sine = turned[:128].T, turned[128:].T
     for ky in range(2):
@@ -593,14 +610,14 @@
     scratch = [
         V((4, 32, 256), F32), V((3, 4, 32, 256), F32), V((4, 32, 256), F32), V((3, WIDTH), BF16), V((WIDTH, WIDTH), BF16),
         V((3, WIDTH), BF16), V((5, 4, 32, 256), F32), V((3, WIDTH, 128), F32),
-        V((2, 2, WIDTH, WIDTH, 128), BF16), V((2, 128, 512), BF16), V((2, 128, 512), BF16), V((2, 512, 128), BF16),
+        V((2, 2, WIDTH, WIDTH, 128), BF16), V((2, 128, 512), BF16), V((2, 128, 512), BF16), V((512, 384), BF16),
         V((2, 256, 512), BF16), V((2, 512, 256), BF16), V((256, 128), BF16),
         field, field, field, field, field, V((3, 5, 8, 384), F32),
         V((2, 5, 8, 128), F32), V((2, 2, 5, 8, 128), F32), V((2, 5, 8, 128), F32), V((4, 5, 8, 128), F32),
-        V((384, 128), F32), coarse, coarse, coarse, coarse, rows, rows, rows, rows, rows, rows,
+        V((384, 128), F32), coarse, coarse, coarse, coarse, V((256, 128), F32), V((256, 128), F32), rows, rows, rows, rows,
         V((2, 2, 3, WIDTH, 128), F32), V((GA, 16, 128), F32), V((GA, 2, 2, WIDTH, 128), F32),
-        V((128, 512), BF16), V((128, 512), BF16), V((512, 512), F32), V((512, 48), F32),
-        V((512, 512), BF16), V((512, 512), BF16), V((4, 128, 128), F32), V((48, 512), F32), V((48, 512), BF16),
+        V((384, 512), BF16), V((512, 512), F32), V((512, 128), F32),
+        V((512, 512), BF16), V((512, 512), BF16), V((4, 128, 128), F32), V((48, 512), F32), V((256, 512), BF16),
         dma((14,)), dma((10,)), dma((10,)), dma((GA,)), dma((GA,)), dma((GA,)), dma((GA,)),
         dma((DEV,)), dma((DEV,)), dma((DEV,)), dma((DEV,)), dma((DEV,)), dma((DEV,)),
         dma((GA,)), dma((GA,)), dma((GA,)), dma((GA,)),

time: 51.6 us -> 48.4 us (0.938)
  Pallas kernels: 50.8 us -> 47.6 us
    pallas_call x1, Pallas kernels: 48.1 us -> 44.9 us  [per_device(): pl.pallas_call(kernel, out_shape=(jax.ShapeDtypeStruct((5, 4, 32, 256), F...]
where the time goes in v2:
time: 48.4 us; the launch traced here: 48.3 us
  Pallas kernels  47.6 us (98%)
  between operations  0.64 us (1%)
    pallas_call x1, Pallas kernels, per_device(): pl.pallas_call(kernel, out_shape=(jax.ShapeDtypeStruct((5, 4, 32, 256), F...  44.9 us
    pallas_call x1, Pallas kernels, per_device(): pl.pallas_call(expand_kernel, out_shape=(jax.ShapeDtypeStruct((2, 2, WIDT...  2.73 us

profile of v2, /device:TPU:1, one launch (start us, length us, event | category | flops | bytes accessed | tf_op | source)
XLA Modules:
  0.0 48.3 jit_solution(7033882654542379853)
XLA Ops:
  0.6 44.9 %shard_map.140 = (f32[5,4,32,256]{3,2,1,0:T(8,128)}, f32[2,2,3,32,128]{4,3,2,1,0:T(8,128)}) custom-call(f32[4,32,256]{2,1,0:T(8,128)} %density_h.1, f32[3,4,32,256]{3,2,1,0:T(8,128)} %velocity_h.1, f32[4,32,256]{2,1,0:T(8,128)} %pressure_h.1, bf16[3,32]{1,0:T(4,128)(2,1)} %lift_h.3, bf16[32,32]{1,0:T(8,128)(2,1)} %pointwise_h.1, bf16[3,32]{1,0:T(4,128)(2,1)} %bitcast.1, ...), custom_call_target="tpu_custom_call" | custom-call | tf_op jit(solution)/shard_map/pallas_call | solution.py:625
  45.6 2.7 %shard_map.141 = (f32[2,2,32,32,128]{4,3,2,1,0:T(8,128)}, f32[5,4,32,256]{3,2,1,0:T(8,128)}) custom-call(bf16[3,32]{1,0:T(4,128)(2,1)} %lift_h.3, f32[2,2,3,32,128]{4,3,2,1,0:T(8,128)} %get-tuple-element.6.t_h, f32[5,4,32,256]{3,2,1,0:T(8,128)} %get-tuple-element.7.state_h), custom_call_target="tpu_custom_call" | custom-call | tf_op jit(solution)/shard_map/pallas_call | solution.py:638

commit v3 on v2

--- a/solution.py
+++ b/solution.py
@@ -19,6 +19,7 @@
 GA = 4
 DEV = 32
 DT = 0.12
+BLOCK = 8
 OFFSETS = sorted(
     ((a, b, c) for a in range(4) for b in range(4) for c in range(2) if a + b + c),
     key=lambda o: (-min(o[0], 4 - o[0]) - min(o[1], 4 - o[1]), o),
@@ -124,20 +125,20 @@
 
 
 def block_rates(src, edge, r0):
-    lane = lax.broadcasted_iota(jnp.int32, (4, 8, 128), 2)
-    odd = lax.broadcasted_iota(jnp.int32, (4, 8, 128), 1) % 2 == 1
+    lane = lax.broadcasted_iota(jnp.int32, (BLOCK, 8, 128), 2)
+    odd = lax.broadcasted_iota(jnp.int32, (BLOCK, 8, 128), 1) % 2 == 1
     last = lane == 127
     base = pl.multiple_of(8 * (r0 - 1), 8)
-    wide = [src[f, pl.ds(base, 48), :].reshape(6, 8, 128) for f in range(5)]
+    wide = [src[f, pl.ds(base, 8 * BLOCK + 16), :].reshape(BLOCK + 2, 8, 128) for f in range(5)]
     v, p, sound = primitives(wide)
     flux, speed = directional(wide, v, p, sound, 1)
     g = faces(
-        [a[:5] for a in wide], [a[1:] for a in wide], [a[:5] for a in flux], [a[1:] for a in flux], speed[:5], speed[1:]
+        [a[:-1] for a in wide], [a[1:] for a in wide], [a[:-1] for a in flux], [a[1:] for a in flux], speed[:-1], speed[1:]
     )
-    total = [a[1:] - a[:4] for a in g]
-    u = [a[1:5] for a in wide]
-    v = [a[1:5] for a in v]
-    p, sound = p[1:5], sound[1:5]
+    total = [a[1:] - a[:-1] for a in g]
+    u = [a[1:-1] for a in wide]
+    v = [a[1:-1] for a in v]
+    p, sound = p[1:-1], sound[1:-1]
 
     flux, speed = directional(u, v, p, sound, 0)
 
@@ -156,7 +157,7 @@
     g = faces(u, [up_y(a) for a in u], flux, [up_y(a) for a in flux], speed, up_y(speed))
     at = pl.multiple_of(8 * r0, 8)
     for f in range(5):
-        outer = edge[f, pl.ds(at, 32), :].reshape(4, 8, 128)
+        outer = edge[f, pl.ds(at, 8 * BLOCK), :].reshape(BLOCK, 8, 128)
         upper = jnp.where(last & odd, outer, g[f])
         wrapped = jnp.where(odd, pltpu.roll(g[f], 1, 1), outer)
         lower = pltpu.roll(jnp.where(last, wrapped, g[f]), 1, 2)
@@ -170,11 +171,11 @@
     new_state_h, t_out,
     density, velocity, pressure, lift, pointwise, project, new_state, lift_wide,
     spectral, fdj, fjd, inv, cx, cxt, pool,
-    u0, ua, ub, acc, edge, rim, own_edge, side_edge, row_edge, corner_edge,
+    u0, ua, ub, uc, acc, edge, rim, own_edge, side_edge, row_edge, corner_edge,
     pooled, snd_in, rcv_in, snd_tg, rcv_tg, snd_x, rcv_x, snd_b, rcv_b, snd_g, rcv_g,
     contracted, modes, grads, rt, slope, made, dp_hi, dp_lo, ft, lpx_ref, pxt_ref,
     load_sem, halo_send, halo_recv, in_send, in_recv, tg_send, tg_recv, x_send, x_recv, b_send, b_recv,
-    g_send, g_recv, xm_send, xm_recv, gm_send, gm_recv,
+    g_send, g_recv, relay, xm_send, xm_recv, gm_send, gm_recv,
 ):
     ga = lax.axis_index("ga")
     dev = lax.axis_index("dev")
@@ -196,57 +197,51 @@
 
     barrier = pltpu.get_barrier_semaphore()
 
-    def greet(s, carry):
-        pl.semaphore_signal(barrier, inc=1, device_id=(ga, lax.rem(dev + s, DEV)), device_id_type=MESH)
-        return carry
-
-    lax.fori_loop(1, DEV, greet, 0)
-    for s in range(1, GA):
-        pl.semaphore_signal(barrier, inc=1, device_id=(lax.rem(ga + s, GA), dev), device_id_type=MESH)
-    for a in (east, west):
-        for b in (south, north):
-            pl.semaphore_signal(barrier, inc=1, device_id=(a, b), device_id_type=MESH)
-
     core, chip_x, chip_y = lax.rem(dev, 2), lax.rem(lax.div(dev, 2), 4), lax.div(dev, 8)
+
+    def at(dy, dx, dc):
+        return lax.rem(chip_y + dy, 4) * 8 + lax.rem(chip_x + dx, 4) * 2 + lax.rem(core + dc, 2)
+
+    beside = jnp.where(core == 1, south, north)
+    line_x = [(ga, at(0, k, 0)) for k in range(1, 4)]
+    first = [(lax.rem(ga + k, GA), dev) for k in range(1, GA)]
+    first += [(ga, at(a, 0, c)) for a in range(4) for c in range(2) if a + c] + line_x + [(ga, beside)]
+    for who in first:
+        pl.semaphore_signal(barrier, inc=1, device_id=who, device_id_type=MESH)
 
     def exchange_rows(snd, rcv, ssem, rsem, unit):
         for dy, dx, dc in OFFSETS:
-            peer = lax.rem(chip_y + dy, 4) * 8 + lax.rem(chip_x + dx, 4) * 2 + lax.rem(core + dc, 2)
+            peer = at(dy, dx, dc)
             pltpu.make_async_remote_copy(
                 src_ref=snd.at[pl.ds(pl.multiple_of(unit * peer, unit), unit)],
                 dst_ref=rcv.at[pl.ds(pl.multiple_of(unit * dev, unit), unit)],
-                send_sem=ssem.at[peer], recv_sem=rsem.at[dev],
+                send_sem=ssem.at[0], recv_sem=rsem.at[0],
                 device_id=(ga, peer), device_id_type=MESH,
             ).start()
         mine = pl.ds(pl.multiple_of(unit * dev, unit), unit)
         rcv[mine, :] = snd[mine, :]
 
     def wait_rows(snd, rcv, ssem, rsem, unit):
-        def go(s, carry):
-            peer = lax.rem(dev + s, DEV)
-            at = pl.ds(pl.multiple_of(unit * peer, unit), unit)
+        whole = pl.ds(0, unit * (DEV - 1))
+        pltpu.make_async_remote_copy(
+            src_ref=snd.at[whole], dst_ref=rcv.at[whole], send_sem=ssem.at[0], recv_sem=rsem.at[0],
+            device_id=(ga, south), device_id_type=MESH,
+        ).wait()
+
+    def start_across(src, dst, ssem, rsem):
+        for k in (2, 1, 3):
+            peer = lax.rem(ga + k, GA)
             pltpu.make_async_remote_copy(
-                src_ref=snd.at[at], dst_ref=rcv.at[at], send_sem=ssem.at[peer], recv_sem=rsem.at[peer],
-                device_id=(ga, peer), device_id_type=MESH,
-            ).wait()
-            return carry
-
-        lax.fori_loop(1, DEV, go, 0)
-
-    def across(s, src, dst, ssem, rsem, arriving):
-        peer = lax.rem(ga + s, GA)
-        return pltpu.make_async_remote_copy(
-            src_ref=src(peer), dst_ref=dst(peer if arriving else ga), send_sem=ssem.at[peer],
-            recv_sem=rsem.at[peer if arriving else ga], device_id=(peer, dev), device_id_type=MESH,
-        )
-
-    def start_across(src, dst, ssem, rsem):
-        for s in (2, 1, 3):
-            across(s, src, dst, ssem, rsem, False).start()
+                src_ref=src(peer), dst_ref=dst.at[ga], send_sem=ssem.at[0], recv_sem=rsem.at[0],
+                device_id=(peer, dev), device_id_type=MESH,
+            ).start()
 
     def wait_across(src, dst, ssem, rsem):
-        for s in (2, 1, 3):
-            across(s, src, dst, ssem, rsem, True).wait()
+        three = dst.at[pl.ds(0, GA - 1)]
+        pltpu.make_async_remote_copy(
+            src_ref=three, dst_ref=three, send_sem=ssem.at[0], recv_sem=rsem.at[0],
+            device_id=(east, dev), device_id_type=MESH,
+        ).wait()
 
     def coarsen(rows, snd):
         hi, lo = split2(rows)
@@ -279,7 +274,10 @@
     loads[0].wait()
     coarsen(jnp.concatenate([velocity[c, p] for p in range(4) for c in range(3)], axis=0), snd_in)
 
-    pl.semaphore_wait(barrier, DEV - 1 + GA - 1 + 4)
+    pl.semaphore_wait(barrier, len(first))
+    second = line_x + [(east, dev), (west, dev)]
+    for who in second:
+        pl.semaphore_signal(relay, inc=1, device_id=who, device_id_type=MESH)
 
     def halo(n, src, dst, target):
         return pltpu.make_async_remote_copy(
@@ -289,17 +287,22 @@
 
     halos = [
         halo(0, u0.at[:, pl.ds(8 * 32, 32)], u0.at[:, pl.ds(0, 32)], (ga, south)),
-        halo(1, u0.at[:, pl.ds(8 * 4, 32)], u0.at[:, pl.ds(8 * 36, 32)], (ga, north)),
-        halo(2, own_edge.at[1], row_edge.at[0], (ga, south)),
-        halo(3, own_edge.at[0], row_edge.at[1], (ga, north)),
-        halo(4, own_edge, side_edge.at[0], (east, dev)),
-        halo(5, own_edge, side_edge.at[1], (west, dev)),
-        halo(6, own_edge.at[1], corner_edge.at[0], (east, south)),
-        halo(7, own_edge.at[0], corner_edge.at[1], (east, north)),
-        halo(8, own_edge.at[1], corner_edge.at[2], (west, south)),
-        halo(9, own_edge.at[0], corner_edge.at[3], (west, north)),
+        halo(0, u0.at[:, pl.ds(8 * 4, 32)], u0.at[:, pl.ds(8 * 36, 32)], (ga, north)),
+        halo(2, own_edge, side_edge.at[0], (east, dev)),
+        halo(2, own_edge, side_edge.at[1], (west, dev)),
+        halo(1, own_edge.at[1], row_edge.at[0], (ga, south)),
+        halo(1, own_edge.at[0], row_edge.at[1], (ga, north)),
     ]
-    in_args = (lambda g: snd_in.at[g], lambda g: rcv_in.at[g], in_send, in_recv)
+    corners = [
+        halo(3, own_edge.at[1], corner_edge.at[0], (east, south)),
+        halo(3, own_edge.at[0], corner_edge.at[1], (east, north)),
+        halo(3, own_edge.at[1], corner_edge.at[2], (west, south)),
+        halo(3, own_edge.at[0], corner_edge.at[3], (west, north)),
+    ]
+    halo_waits = [
+        halo(n, a, a, (ga, south)) for n, a in enumerate((u0.at[:, pl.ds(0, 64)], row_edge, side_edge, corner_edge))
+    ]
+    in_args = (lambda g: snd_in.at[g], rcv_in, in_send, in_recv)
     start_across(*in_args)
     for c in halos:
         c.start()
@@ -342,6 +345,10 @@
     lpx_ref[...] = spread(nn(lp_hi, tile_o) + nn(lp_lo, tile_o))
     spread_out = jnp.concatenate([spread(nn(project[...], tile_o)), jnp.zeros((80, 512), F32)], axis=0)
     pxt_ref[...] = jnp.concatenate([spread_out, spread_out], axis=0).astype(BF16)
+
+    pl.semaphore_wait(relay, len(second))
+    for c in corners:
+        c.start()
 
     wait_across(*in_args)
     loads[2].wait()
@@ -357,10 +364,10 @@
     x_args = (snd_x, rcv_x, x_send, x_recv, 8)
     exchange_rows(*x_args)
 
-    for c in halos:
+    for c in halo_waits:
         c.wait()
     sub1 = lax.broadcasted_iota(jnp.int32, (8, 128), 0)
-    even, first = sub1 % 2 == 0, lane1 % 8 < 4
+    even, outside = sub1 % 2 == 0, lane1 % 8 < 4
     low = lane1 < 64
     for f in range(5):
         own = [own_edge[0, f], own_edge[1, f], jnp.where(low, row_edge[1, f], row_edge[0, f])]
@@ -369,11 +376,11 @@
         for n in range(3):
             rim[0, f, :, 128 * n : 128 * n + 128] = jnp.where(
                 even,
-                jnp.where(first, pltpu.roll(left[n], 7, 0), own[n]),
-                jnp.where(first, own[n], pltpu.roll(right[n], 1, 0)),
+                jnp.where(outside, pltpu.roll(left[n], 7, 0), own[n]),
+                jnp.where(outside, own[n], pltpu.roll(right[n], 1, 0)),
             )
 
-    def stage(src, dst, ahead, gain, first_row, blocks, first_stage, rim_src, rim_dst):
+    def stage(src, dst, ahead, first_row, last_row, rim_src, rim_dst):
         total, along_y = rim_rates([rim[rim_src, f] for f in range(5)])
         for f in range(5):
             if rim_dst is not None:
@@ -385,24 +392,21 @@
                     )
 
         def block(n, carry):
-            r0 = first_row + 4 * n
-            if first_stage:
-                r0 = jnp.minimum(r0, 35)
+            r0 = jnp.minimum(first_row + BLOCK * n, last_row + 1 - BLOCK)
             total = block_rates(src, edge, r0)
-            at = pl.ds(pl.multiple_of(8 * r0, 8), 32)
+            at = pl.ds(pl.multiple_of(8 * r0, 8), 8 * BLOCK)
             for f in range(5):
-                t = total[f].reshape(32, 128)
-                start = u0[f, at, :]
+                t = total[f].reshape(8 * BLOCK, 128)
                 if dst is not None:
-                    dst[f, at, :] = start - (0.5 * ahead) * t
-                old = start if first_stage else acc[f, at, :]
-                acc[f, at, :] = old - (0.5 * gain) * t
+                    dst[f, at, :] = u0[f, at, :] - (0.5 * ahead) * t
+                else:
+                    mean = (ua[f, at, :] + 2.0 * ub[f, at, :] + uc[f, at, :] - u0[f, at, :]) * (1.0 / 3.0)
+                    acc[f, at, :] = mean - (DT / 12.0) * t
             return carry
 
-        lax.fori_loop(0, blocks, block, 0)
-
-    stage(u0, ua, 0.5 * DT, DT / 6, 1, 10, True, 0, 1)
-    stage(ua, ub, 0.5 * DT, DT / 3, 2, 9, False, 1, 2)
+        lax.fori_loop(0, -(-(last_row + 1 - first_row) // BLOCK), block, 0)
+
+    stage(u0, ua, 0.5 * DT, 1, 38, 0, 1)
 
     wait_rows(*x_args)
     loads[3].wait()
@@ -419,7 +423,7 @@
             modes[ga, 8 * ky + 2 * c : 8 * ky + 2 * c + 1, :] = cosine[r : r + 1] + sine[r + 1 : r + 2]
             modes[ga, 8 * ky + 2 * c + 1 : 8 * ky + 2 * c + 2, :] = cosine[r + 1 : r + 2] - sine[r : r + 1]
         modes[ga, 8 * ky + 6 : 8 * ky + 8, :] = jnp.zeros((2, 128), F32)
-    modes_args = (lambda g: modes.at[ga], lambda g: modes.at[g], xm_send, xm_recv)
+    modes_args = (lambda g: modes.at[ga], modes, xm_send, xm_recv)
     start_across(*modes_args)
     mine = modes[ga]
     rows = []
@@ -439,8 +443,9 @@
     b_args = (snd_b, rcv_b, b_send, b_recv, 16)
     exchange_rows(*b_args)
 
-    stage(ub, ua, DT, DT / 3, 2, 9, False, 2, 1)
-    stage(ua, None, DT, DT / 6, 4, 8, False, 1, None)
+    stage(ua, ub, 0.5 * DT, 2, 37, 1, 2)
+    stage(ub, uc, DT, 3, 36, 2, 1)
+    stage(uc, None, DT, 4, 35, 1, None)
 
     after = []
     for p in range(4):
@@ -458,7 +463,7 @@
     coarsen(jnp.concatenate(after, axis=0), snd_tg)
     state_copy = pltpu.make_async_copy(new_state, new_state_h, load_sem.at[13])
     state_copy.start()
-    tg_args = (lambda g: snd_tg.at[g], lambda g: rcv_tg.at[g], tg_send, tg_recv)
+    tg_args = (lambda g: snd_tg.at[g], rcv_tg, tg_send, tg_recv)
     start_across(*tg_args)
     rcv_tg[ga] = snd_tg[ga]
 
@@ -539,7 +544,7 @@
         re, im = slice(64 * ky, 64 * ky + 32), slice(64 * ky + 32, 64 * ky + 64)
         grads[ga, ky, 0] = cosine[re] + sine[im]
         grads[ga, ky, 1] = cosine[im] - sine[re]
-    grads_args = (lambda g: grads.at[ga], lambda g: grads.at[g], gm_send, gm_recv)
+    grads_args = (lambda g: grads.at[ga], grads, gm_send, gm_recv)
     start_across(*grads_args)
     wait_across(*modes_args)
     wait_across(*grads_args)
@@ -564,7 +569,7 @@
     ]
     for c in loads:
         c.start()
-    forward = pltpu.make_async_copy(state, new_state_h, sem.at[19])
+    forward = pltpu.make_async_copy(state, new_state_h, sem.at[4])
     loads[0].wait()
     for c in range(3):
         lift_wide[c] = widened(lift[...], c)
@@ -573,7 +578,7 @@
     def stretch(n):
         ky, rest = n // 8, n % 8
         part, rows = rest // 4, pl.ds(8 * (rest % 4), 8)
-        return pltpu.make_async_copy(out.at[ky, part, rows], out_h.at[ky, part, rows], sem.at[3 + n])
+        return pltpu.make_async_copy(out.at[ky, part, rows], out_h.at[ky, part, rows], sem.at[3])
 
     def body(n, carry):
         ky, rest = n // 8, n % 8
@@ -592,11 +597,7 @@
     forward.start()
     lax.fori_loop(4, 16, body, 0)
 
-    def done(n, carry):
-        stretch(n).wait()
-        return carry
-
-    lax.fori_loop(0, 16, done, 0)
+    pltpu.make_async_copy(out, out_h, sem.at[3]).wait()
     forward.wait()
 
 
@@ -612,15 +613,15 @@
         V((3, WIDTH), BF16), V((5, 4, 32, 256), F32), V((3, WIDTH, 128), F32),
         V((2, 2, WIDTH, WIDTH, 128), BF16), V((2, 128, 512), BF16), V((2, 128, 512), BF16), V((512, 384), BF16),
         V((2, 256, 512), BF16), V((2, 512, 256), BF16), V((256, 128), BF16),
-        field, field, field, field, field, V((3, 5, 8, 384), F32),
+        field, field, field, field, field, field, V((3, 5, 8, 384), F32),
         V((2, 5, 8, 128), F32), V((2, 2, 5, 8, 128), F32), V((2, 5, 8, 128), F32), V((4, 5, 8, 128), F32),
         V((384, 128), F32), coarse, coarse, coarse, coarse, V((256, 128), F32), V((256, 128), F32), rows, rows, rows, rows,
         V((2, 2, 3, WIDTH, 128), F32), V((GA, 16, 128), F32), V((GA, 2, 2, WIDTH, 128), F32),
         V((384, 512), BF16), V((512, 512), F32), V((512, 128), F32),
         V((512, 512), BF16), V((512, 512), BF16), V((4, 128, 128), F32), V((48, 512), F32), V((256, 512), BF16),
-        dma((14,)), dma((10,)), dma((10,)), dma((GA,)), dma((GA,)), dma((GA,)), dma((GA,)),
-        dma((DEV,)), dma((DEV,)), dma((DEV,)), dma((DEV,)), dma((DEV,)), dma((DEV,)),
-        dma((GA,)), dma((GA,)), dma((GA,)), dma((GA,)),
+        dma((14,)), dma((4,)), dma((4,)), dma((1,)), dma((1,)), dma((1,)), dma((1,)),
+        dma((1,)), dma((1,)), dma((1,)), dma((1,)), dma((1,)), dma((1,)),
+        pltpu.SemaphoreType.REGULAR, dma((1,)), dma((1,)), dma((1,)), dma((1,)),
     ]
     new_state, t = pl.pallas_call(
         kernel,
@@ -645,7 +646,7 @@
         out_specs=(hbm, hbm),
         scratch_shapes=[
             V((3, WIDTH), BF16), V((2, 2, 3, WIDTH, 128), F32), V((5, 4, 32, 256), F32), V((3, WIDTH, 128), F32),
-            V((2, 2, WIDTH, WIDTH, 128), F32), dma((20,)),
+            V((2, 2, WIDTH, WIDTH, 128), F32), dma((5,)),
         ],
         compiler_params=pltpu.CompilerParams(vmem_limit_bytes=VMEM_BYTES),
     )(lift, t, new_state)

time: 48.4 us -> 45 us (0.930)
  Pallas kernels: 47.6 us -> 44.2 us
    pallas_call x1, Pallas kernels: 44.9 us -> 41.6 us  [per_device(): pl.pallas_call(kernel, out_shape=(jax.ShapeDtypeStruct((5, 4, 32, 256), F...]
where the time goes in v3:
time: 45 us; the launch traced here: 44.9 us
  Pallas kernels  44.2 us (98%)
  between operations  0.64 us (1%)
    pallas_call x1, Pallas kernels, per_device(): pl.pallas_call(kernel, out_shape=(jax.ShapeDtypeStruct((5, 4, 32, 256), F...  41.6 us
    pallas_call x1, Pallas kernels, per_device(): pl.pallas_call(expand_kernel, out_shape=(jax.ShapeDtypeStruct((2, 2, WIDT...  2.59 us

profile of v3, /device:TPU:1, one launch (start us, length us, event | category | flops | bytes accessed | tf_op | source)
XLA Modules:
  0.0 44.9 jit_solution(6694359716251419155)
XLA Ops:
  0.6 41.6 %shard_map.140 = (f32[5,4,32,256]{3,2,1,0:T(8,128)}, f32[2,2,3,32,128]{4,3,2,1,0:T(8,128)}) custom-call(f32[4,32,256]{2,1,0:T(8,128)} %density_h.1, f32[3,4,32,256]{3,2,1,0:T(8,128)} %velocity_h.1, f32[4,32,256]{2,1,0:T(8,128)} %pressure_h.1, bf16[3,32]{1,0:T(4,128)(2,1)} %lift_h.3, bf16[32,32]{1,0:T(8,128)(2,1)} %pointwise_h.1, bf16[3,32]{1,0:T(4,128)(2,1)} %bitcast.1, ...), custom_call_target="tpu_custom_call" | custom-call | tf_op jit(solution)/shard_map/pallas_call | solution.py:626
  42.3 2.6 %shard_map.141 = (f32[2,2,32,32,128]{4,3,2,1,0:T(8,128)}, f32[5,4,32,256]{3,2,1,0:T(8,128)}) custom-call(bf16[3,32]{1,0:T(4,128)(2,1)} %lift_h.3, f32[2,2,3,32,128]{4,3,2,1,0:T(8,128)} %get-tuple-element.6.t_h, f32[5,4,32,256]{3,2,1,0:T(8,128)} %get-tuple-element.7.state_h), custom_call_target="tpu_custom_call" | custom-call | tf_op jit(solution)/shard_map/pallas_call | solution.py:639

commit v4 on v3

--- a/solution.py
+++ b/solution.py
@@ -364,23 +364,16 @@
     x_args = (snd_x, rcv_x, x_send, x_recv, 8)
     exchange_rows(*x_args)
 
-    for c in halo_waits:
-        c.wait()
     sub1 = lax.broadcasted_iota(jnp.int32, (8, 128), 0)
     even, outside = sub1 % 2 == 0, lane1 % 8 < 4
     low = lane1 < 64
-    for f in range(5):
-        own = [own_edge[0, f], own_edge[1, f], jnp.where(low, row_edge[1, f], row_edge[0, f])]
-        left = [side_edge[0, 0, f], side_edge[0, 1, f], jnp.where(low, corner_edge[1, f], corner_edge[0, f])]
-        right = [side_edge[1, 0, f], side_edge[1, 1, f], jnp.where(low, corner_edge[3, f], corner_edge[2, f])]
-        for n in range(3):
-            rim[0, f, :, 128 * n : 128 * n + 128] = jnp.where(
-                even,
-                jnp.where(outside, pltpu.roll(left[n], 7, 0), own[n]),
-                jnp.where(outside, own[n], pltpu.roll(right[n], 1, 0)),
-            )
-
-    def stage(src, dst, ahead, first_row, last_row, rim_src, rim_dst):
+
+    def fill_rim(n, f, own, left, right):
+        rim[0, f, :, 128 * n : 128 * n + 128] = jnp.where(
+            even, jnp.where(outside, pltpu.roll(left, 7, 0), own), jnp.where(outside, own, pltpu.roll(right, 1, 0))
+        )
+
+    def stage(src, dst, ahead, first_row, last_row, rim_src, rim_dst, stride=BLOCK):
         total, along_y = rim_rates([rim[rim_src, f] for f in range(5)])
         for f in range(5):
             if rim_dst is not None:
@@ -392,7 +385,7 @@
                     )
 
         def block(n, carry):
-            r0 = jnp.minimum(first_row + BLOCK * n, last_row + 1 - BLOCK)
+            r0 = jnp.minimum(first_row + stride * n, last_row + 1 - BLOCK)
             total = block_rates(src, edge, r0)
             at = pl.ds(pl.multiple_of(8 * r0, 8), 8 * BLOCK)
             for f in range(5):
@@ -404,9 +397,23 @@
                     acc[f, at, :] = mean - (DT / 12.0) * t
             return carry
 
-        lax.fori_loop(0, -(-(last_row + 1 - first_row) // BLOCK), block, 0)
-
-    stage(u0, ua, 0.5 * DT, 1, 38, 0, 1)
+        lax.fori_loop(0, -(-(last_row + 1 - first_row) // stride), block, 0)
+
+    halo_waits[2].wait()
+    for f in range(5):
+        for n in range(2):
+            fill_rim(n, f, own_edge[n, f], side_edge[0, n, f], side_edge[1, n, f])
+        fill_rim(2, f, own_edge[0, f], side_edge[0, 0, f], side_edge[1, 0, f])
+    stage(u0, ua, 0.5 * DT, 5, 34, 0, None)
+    for n in (0, 1, 3):
+        halo_waits[n].wait()
+    for f in range(5):
+        fill_rim(
+            2, f, jnp.where(low, row_edge[1, f], row_edge[0, f]),
+            jnp.where(low, corner_edge[1, f], corner_edge[0, f]), jnp.where(low, corner_edge[3, f], corner_edge[2, f]),
+        )
+    stage(u0, ua, 0.5 * DT, 1, 38, 0, 1, 30)
+    stage(ua, ub, 0.5 * DT, 2, 37, 1, 2)
 
     wait_rows(*x_args)
     loads[3].wait()
@@ -443,7 +450,6 @@
     b_args = (snd_b, rcv_b, b_send, b_recv, 16)
     exchange_rows(*b_args)
 
-    stage(ua, ub, 0.5 * DT, 2, 37, 1, 2)
     stage(ub, uc, DT, 3, 36, 2, 1)
     stage(uc, None, DT, 4, 35, 1, None)
 

time: 45 us -> 43.3 us (0.962)
  Pallas kernels: 44.2 us -> 42.6 us
    pallas_call x1, Pallas kernels: 41.6 us -> 40 us  [per_device(): pl.pallas_call(kernel, out_shape=(jax.ShapeDtypeStruct((5, 4, 32, 256), F...]
where the time goes in v4:
time: 43.3 us; the launch traced here: 43.2 us
  Pallas kernels  42.6 us (98%)
  between operations  0.64 us (1%)
    pallas_call x1, Pallas kernels, per_device(): pl.pallas_call(kernel, out_shape=(jax.ShapeDtypeStruct((5, 4, 32, 256), F...  40 us
    pallas_call x1, Pallas kernels, per_device(): pl.pallas_call(expand_kernel, out_shape=(jax.ShapeDtypeStruct((2, 2, WIDT...  2.59 us

profile of v4, /device:TPU:1, one launch (start us, length us, event | category | flops | bytes accessed | tf_op | source)
XLA Modules:
  0.0 43.2 jit_solution(8678614136763016003)
XLA Ops:
  0.6 40.0 %shard_map.140 = (f32[5,4,32,256]{3,2,1,0:T(8,128)}, f32[2,2,3,32,128]{4,3,2,1,0:T(8,128)}) custom-call(f32[4,32,256]{2,1,0:T(8,128)} %density_h.1, f32[3,4,32,256]{3,2,1,0:T(8,128)} %velocity_h.1, f32[4,32,256]{2,1,0:T(8,128)} %pressure_h.1, bf16[3,32]{1,0:T(4,128)(2,1)} %lift_h.3, bf16[32,32]{1,0:T(8,128)(2,1)} %pointwise_h.1, bf16[3,32]{1,0:T(4,128)(2,1)} %bitcast.1, ...), custom_call_target="tpu_custom_call" | custom-call | tf_op jit(solution)/shard_map/pallas_call | solution.py:632
  40.6 2.6 %shard_map.141 = (f32[2,2,32,32,128]{4,3,2,1,0:T(8,128)}, f32[5,4,32,256]{3,2,1,0:T(8,128)}) custom-call(bf16[3,32]{1,0:T(4,128)(2,1)} %lift_h.3, f32[2,2,3,32,128]{4,3,2,1,0:T(8,128)} %get-tuple-element.6.t_h, f32[5,4,32,256]{3,2,1,0:T(8,128)} %get-tuple-element.7.state_h), custom_call_target="tpu_custom_call" | custom-call | tf_op jit(solution)/shard_map/pallas_call | solution.py:645

commit v5 on v4

--- a/solution.py
+++ b/solution.py
@@ -458,20 +458,21 @@
         parts = []
         for h in range(2):
             where = pl.ds(32 + 2 * p + h, 32, stride=8)
-            cols = slice(128 * h, 128 * h + 128)
             u = [acc[f, where, :] for f in range(5)]
-            for f in range(5):
-                new_state[f, p, :, cols] = u[f]
             inv_rho = 1.0 / u[0]
             parts.append([u[1 + c] * inv_rho for c in range(3)])
         for c in range(3):
             after.append(jnp.concatenate([parts[0][c], parts[1][c]], axis=1))
     coarsen(jnp.concatenate(after, axis=0), snd_tg)
-    state_copy = pltpu.make_async_copy(new_state, new_state_h, load_sem.at[13])
-    state_copy.start()
     tg_args = (lambda g: snd_tg.at[g], rcv_tg, tg_send, tg_recv)
     start_across(*tg_args)
     rcv_tg[ga] = snd_tg[ga]
+    for p in range(4):
+        for h in range(2):
+            for f in range(5):
+                new_state[f, p, :, 128 * h : 128 * h + 128] = acc[f, pl.ds(32 + 2 * p + h, 32, stride=8), :]
+    state_copy = pltpu.make_async_copy(new_state, new_state_h, load_sem.at[13])
+    state_copy.start()
 
     lpx_hi, lpx_lo = split2(lpx_ref[...])
 
@@ -510,7 +511,7 @@
         made[at, :] = nt(hi, pxt_ref[:128]) + nt(lo, pxt_ref[:128])
         return carry
 
-    lax.fori_loop(0, GA, forward, 0)
+    lax.fori_loop(0, GA, forward, 0, unroll=True)
 
     wait_across(*tg_args)
 
@@ -523,7 +524,7 @@
         dp_lo[at, :] = lo
         return carry
 
-    lax.fori_loop(0, GA, backward, 0)
+    lax.fori_loop(0, GA, backward, 0, unroll=True)
     loads[6].wait()
     for t in range(2):
         cols = slice(256 * t, 256 * t + 256)

time: 43.3 us -> 41.9 us (0.968)
  Pallas kernels: 42.6 us -> 41.1 us
    pallas_call x1, Pallas kernels: 40 us -> 38.5 us  [per_device(): pl.pallas_call(kernel, out_shape=(jax.ShapeDtypeStruct((5, 4, 32, 256), F...]
where the time goes in v5:
time: 41.9 us; the launch traced here: 41.7 us
  Pallas kernels  41.1 us (98%)
  between operations  0.64 us (2%)
    pallas_call x1, Pallas kernels, per_device(): pl.pallas_call(kernel, out_shape=(jax.ShapeDtypeStruct((5, 4, 32, 256), F...  38.5 us
    pallas_call x1, Pallas kernels, per_device(): pl.pallas_call(expand_kernel, out_shape=(jax.ShapeDtypeStruct((2, 2, WIDT...  2.59 us

profile of v5, /device:TPU:1, one launch (start us, length us, event | category | flops | bytes accessed | tf_op | source)
XLA Modules:
  0.0 41.7 jit_solution(6827095127766035202)
XLA Ops:
  0.6 38.5 %shard_map.140 = (f32[5,4,32,256]{3,2,1,0:T(8,128)}, f32[2,2,3,32,128]{4,3,2,1,0:T(8,128)}) custom-call(f32[4,32,256]{2,1,0:T(8,128)} %density_h.1, f32[3,4,32,256]{3,2,1,0:T(8,128)} %velocity_h.1, f32[4,32,256]{2,1,0:T(8,128)} %pressure_h.1, bf16[3,32]{1,0:T(4,128)(2,1)} %lift_h.3, bf16[32,32]{1,0:T(8,128)(2,1)} %pointwise_h.1, bf16[3,32]{1,0:T(4,128)(2,1)} %bitcast.1, ...), custom_call_target="tpu_custom_call" | custom-call | tf_op jit(solution)/shard_map/pallas_call | solution.py:633
  39.1 2.6 %shard_map.141 = (f32[2,2,32,32,128]{4,3,2,1,0:T(8,128)}, f32[5,4,32,256]{3,2,1,0:T(8,128)}) custom-call(bf16[3,32]{1,0:T(4,128)(2,1)} %lift_h.3, f32[2,2,3,32,128]{4,3,2,1,0:T(8,128)} %get-tuple-element.6.t_h, f32[5,4,32,256]{3,2,1,0:T(8,128)} %get-tuple-element.7.state_h), custom_call_target="tpu_custom_call" | custom-call | tf_op jit(solution)/shard_map/pallas_call | solution.py:646
